TPU v7x, 256 devices: a whole 4x4x8 slice. The times are simulated.
256 devices in a mesh: dp: 4 (over y), row: 4 (over z_lo, core), col: 16 (over x, z_hi).
Axes of the slice: x: 4, y: 4, z: 8 (z_hi: 4, z_lo: 2; z = z_hi * 2 + z_lo), core: 2. Of those that a mesh axis runs over, the one named last changes fastest.
Arguments:
- weight: float32 [512, 73728], P('row', 'col'), may hold values from -6 to 6
- grad_parts: bfloat16 [4, 512, 73728], P('dp', 'row', 'col'), may hold values from -200 to 200
- row_moment: float32 [512], P('row'), may hold values from 0.2 to 20
- col_moment: float32 [73728], P('col'), may hold values from 0.2 to 20
Outputs:
- new_weight: float32 [512, 73728], P('row', 'col')
- update: float32 [512, 73728], P('row', 'col')
- row_new: float32 [512], P('row')
- col_new: float32 [73728], P('col')
- clip_factor: float32 [], replicated
All inputs are finite; a program needn't handle non-finite values.
Results may differ from a plain program's by a relative error of at most 0.0003.
Values sent between devices are 32-bit elements; how exact they have to be, the bound alone decides.
A program may use at most 64 MiB of HBM per device.

v0:
```python
import jax
import jax.numpy as jnp
from jax import lax
from jax.sharding import PartitionSpec as P

decay_rate = 0.5
eps_one = 1e-30
eps_two = 0.001
learn_rate = 0.01
clip_level = 1.0


def body(weight, grad_parts, row_moment, col_moment):
    local = grad_parts[0].astype(jnp.float32)
    rows_all = weight.shape[0] * lax.axis_size("row")
    cols_all = weight.shape[1] * lax.axis_size("col")
    entries = rows_all * cols_all
    grad = lax.psum(local, "dp")
    squared = grad * grad
    weight_local = jnp.sum(weight * weight)
    row_sum = lax.psum(jnp.sum(squared, axis=1), "col")
    row_new = decay_rate * row_moment + (1.0 - decay_rate) * (row_sum / cols_all + eps_one)
    col_sum = lax.psum(jnp.sum(squared, axis=0), "row")
    col_new = decay_rate * col_moment + (1.0 - decay_rate) * (col_sum / rows_all + eps_one)
    row_total = lax.psum(jnp.sum(row_new), "row")
    row_mean = row_total / rows_all
    raw = grad / jnp.sqrt(row_new[:, None] * col_new[None, :] / row_mean)
    raw_local = jnp.sum(raw * raw)
    raw_total, weight_total = lax.psum((raw_local, weight_local), ("row", "col"))
    clip = jnp.maximum(1.0, jnp.sqrt(raw_total / entries) / clip_level)
    update = raw / clip
    step_size = learn_rate * jnp.maximum(eps_two, jnp.sqrt(weight_total / entries))
    new_weight = weight - step_size * update
    return (new_weight, update, row_new, col_new, clip)


def solution(mesh):
    return jax.shard_map(
        body,
        mesh=mesh,
        in_specs=(P("row", "col"), P("dp", "row", "col"), P("row"), P("col")),
        out_specs=(P("row", "col"), P("row", "col"), P("row"), P("col"), P()),
        check_vma=False,
    )
```

profile of v0, /device:TPU:32, one launch (start us, length us, event | category | flops | bytes accessed | tf_op | source)
XLA Modules:
  0.0 310.0 jit_solution(18184442644516824564)
XLA Ops:
  7.2 0.0 copy-start.1
  7.2 0.0 all-reduce.4.cloned.1.call-start
  7.2 3.1 bitcast_convert_fusion
  10.3 0.0 all-reduce.4.cloned.1.call-update
  10.3 0.0 copy-done.1
  10.3 0.0 copy-start.5
  10.3 0.0 copy-start.3
  10.3 1.2 multiply_reduce_fusion.1
  11.6 70.2 %all-reduce.4.cloned.1.call-done = f32[128,4608]{1,0:T(8,128)} async-done(((f32[128,4608]{1,0:T(8,128)}), f32[128,4608]{1,0:T(8,128)}) %all-reduce.4.cloned.1.call-update) | async-done | bytes 2359312 | tf_op jit(solution)/shard_map/psum | solution.py:18
  81.7 0.0 copy-start
  81.7 2.1 multiply_reduce_fusion.2
  83.9 44.4 %psum.44 = f32[128]{0:T(128)S(1)} all-reduce(f32[128]{0:T(128)S(1)} %get-tuple-element.6), channel_id=1, replica_groups=mesh['dp'=4,'row'=4,'col'=16] {'col'}, use_global_device_ids=true, to_apply=%region_4.0 | all-reduce | flops 128 | bytes 1024 | tf_op jit(solution)/shard_map/psum | solution.py:21
  128.3 0.0 copy-done.5
  128.3 0.6 fusion
  128.9 0.0 copy-start.4
  128.9 10.3 %all-reduce.1 = (f32[]{:T(128)}, f32[4608]{0:T(1024)S(1)}) all-reduce(f32[]{:T(128)} %get-tuple-element.13, f32[4608]{0:T(1024)S(1)} %get-tuple-element.5), channel_id=1, replica_groups=mesh['dp'=4,'row'=4,'col'=16] {'row'}, use_global_device_ids=true, to_apply=%region_8.0 | all-reduce | flops 4609 | bytes 36872 | tf_op jit(solution)/shard_map/psum | solution.py:25
  139.8 0.0 copy-done.3
  139.8 0.0 copy-start.2
  139.9 0.0 copy-done
  139.9 1.3 multiply_reduce_fusion
  141.2 154.8 %all-reduce = (f32[]{:T(128)}, f32[]{:T(128)}) all-reduce(f32[]{:T(128)} %multiply_reduce_fusion, f32[]{:T(128)} %multiply_reduce_fusion.1), channel_id=1, replica_groups=mesh['dp'=4,'row'=4,'col'=16] {'row','col'}, use_global_device_ids=true, to_apply=%region_10.0 | all-reduce | flops 2 | bytes 16 | tf_op jit(solution)/shard_map/psum | solution.py:29
  297.4 4.7 %multiply_subtract_fusion = (f32[128,4608]{1,0:T(8,128)}, f32[128,4608]{1,0:T(8,128)}) fusion(f32[128,4608]{1,0:T(8,128)} %param.4, f32[]{:T(128)S(6)} %mul_shard_map.3, f32[]{:T(128)} %max.3, f32[128,4608]{1,0:T(8,128)S(1)} %copy-done, f32[]{:T(128)S(6)} %div.42, f32[4608]{0:T(1024)S(1)} %add_multiply_fusion, f32[128]{0:T(128)S(1)} %get-tuple-element.14), kind=kLoop, calls=%fused_computation | loop fusion | flops 3538944 | bytes 9456140 | tf_op jit(solution)/shard_map/sub | solution.py:33
  302.0 0.0 copy-done.4
  302.0 0.0 copy-done.2
  (1 shorter events, 0.0 us)
Async XLA Ops:
  7.2 3.1 %copy-start.1 = (f32[128,4608]{1,0:T(8,128)S(1)}, f32[128,4608]{1,0:T(8,128)}, u32[]{:S(2)}) copy-start(f32[128,4608]{1,0:T(8,128)} %param.4) | copy-start | bytes 7077892
  7.2 74.6 %all-reduce.4.cloned.1.call-start = ((), (), s32[]{:S(2)}) async-start(), calls=%async_computation | async-start | bytes 4718592 | tf_op jit(solution)/shard_map/psum | solution.py:18
  10.3 118.0 %copy-start.5 = (f32[128]{0:T(128)S(1)}, f32[128]{0:T(128)}, u32[]{:S(2)}) copy-start(f32[128]{0:T(128)} %param.6) | copy-start | bytes 1540
  10.3 129.5 %copy-start.3 = (f32[4608]{0:T(1024)S(1)}, f32[4608]{0:T(1024)}, u32[]{:S(2)}) copy-start(f32[4608]{0:T(1024)} %param.7) | copy-start | bytes 55300
  81.7 58.1 %copy-start = (f32[128,4608]{1,0:T(8,128)S(1)}, f32[128,4608]{1,0:T(8,128)}, u32[]{:S(2)}) copy-start(f32[128,4608]{1,0:T(8,128)} %all-reduce.4.cloned.1.call-done) | copy-start | bytes 7077892
  128.9 173.1 %copy-start.4 = (f32[128]{0:T(128)}, f32[128]{0:T(128)S(1)}, u32[]{:S(2)}) copy-start(f32[128]{0:T(128)S(1)} %get-tuple-element.14) | copy-start | bytes 1540
  139.8 162.2 %copy-start.2 = (f32[4608]{0:T(1024)}, f32[4608]{0:T(1024)S(1)}, u32[]{:S(2)}) copy-start(f32[4608]{0:T(1024)S(1)} %add_multiply_fusion) | copy-start | bytes 55300
Sparse Core Ops, SparseCore 0:
  11.0 70.7 all-reduce.3
where the time goes:
time: 310 us
  blocking collectives  209 us (67%)
  waiting for transfers between devices  70.2 us (23%)
  between operations  17.3 us (6%)
  other arithmetic  13 us (4%)
    psum x1, blocking collectives, body(): lax.psum((raw_local, weight_local), ('row', 'col'))  155 us
    psum x1, waiting for transfers between devices, body(): grad = lax.psum(local, 'dp')  70.2 us
    psum x1, blocking collectives, body(): row_sum = lax.psum(jnp.sum(squared, axis=1), 'col')  44.4 us
    psum x1, blocking collectives, body(): row_total = lax.psum(jnp.sum(row_new), 'row')  10.3 us
  transfers between devices with their start and end apart: 1, of which 1 were waited for; matrix products, arithmetic and copies ran while one was open for 0% of the time, Pallas kernels for 0%

commit v1 on v0

v1 whole, which is shorter than its diff:
```python
import functools

import jax
import jax.numpy as jnp
from jax import lax
from jax.experimental import pallas as pl
from jax.experimental.pallas import tpu as pltpu
from jax.sharding import PartitionSpec as P

decay_rate = 0.5
eps_one = 1e-30
eps_two = 0.001
learn_rate = 0.01
clip_level = 1.0

MESH = pl.DeviceIdType.MESH
f32 = jnp.float32
CHUNKS = 4
PA, PB, PC, PD, PX, PE = range(6)


def exchange_kernel(sizes, grad_hbm, weight_hbm, rowm_hbm, colm_hbm,
                    full, held, col_all, row_new, row_scale, col_scale, scal,
                    own, s_opp, s_right, s_left, r_opp, r_left, r_right, lanes,
                    rowm, colm, col_old, col_parts, row_parts, scal_parts,
                    load_sem, send_sem, recv_sem, xs_sem, xr_sem, cs_sem, cr_sem):
    n_dp, n_row, n_col, splits = sizes
    rows, width = own.shape[1], own.shape[2]
    half = rows // 2
    step = half // CHUNKS
    rows_all = rows * n_row
    cols_all = width * n_dp * n_col
    entries = float(rows_all) * float(cols_all)
    y, r, c = lax.axis_index("dp"), lax.axis_index("row"), lax.axis_index("col")
    right, opp, left = lax.rem(y + 1, 4), lax.rem(y + 2, 4), lax.rem(y + 3, 4)

    groups = [("dp", y, n_dp, lambda i: i)]
    for size, stride in splits:
        at = lax.rem(c // stride, size)
        groups.append(("col", at, size, functools.partial(lambda s, a, i: c + (i - a) * s, stride, at)))
    row_group = ("row", r, n_row, lambda i: i)

    def peers(group):
        axis, at, size, index = group
        return [(d, {axis: index(lax.rem(at + d, size))}, lax.rem(at + size - d, size)) for d in range(1, size)]

    loads = {}
    for slot, q in ((2, opp), (1, right), (3, left), (0, y)):
        loads[slot] = pltpu.make_async_copy(
            grad_hbm.at[0, :, pl.ds(pl.multiple_of(q * width, 128), width)], own.at[slot], load_sem.at[slot])
        loads[slot].start()
    barrier = pltpu.get_barrier_semaphore()
    count = 0
    for group in groups + [row_group]:
        for _, dev, _ in peers(group):
            pl.semaphore_signal(barrier, inc=1, device_id=dev, device_id_type=MESH)
            count += 1
    wloads = []
    for q in range(4):
        wloads.append(pltpu.make_async_copy(
            weight_hbm.at[:, pl.ds(q * width, width)], held.at[q], load_sem.at[4 + q]))
        wloads[-1].start()
    load_row = pltpu.make_async_copy(rowm_hbm, rowm, load_sem.at[8])
    load_col = pltpu.make_async_copy(colm_hbm, colm, load_sem.at[9])
    load_row.start()
    load_col.start()

    def at(h, k):
        return pl.ds(h * half + k * step, step)

    def bulk(phase, d, k):
        if phase == PA:
            src, dst = s_opp.at[at(d, k)], r_opp.at[at(d, k)]
        elif phase in (PB, PC):
            h = d if phase == PC else 1 - d
            src, dst = ((s_right, r_left), (s_left, r_right))[d]
            src, dst = src.at[at(h, k)], dst.at[at(h, k)]
        else:
            h = 1 - d if phase == PX else d
            q = y if phase != PE else (left, right)[d]
            src = dst = full.at[q, at(h, k)]
        return pltpu.make_async_remote_copy(
            src_ref=src, dst_ref=dst, send_sem=send_sem.at[phase, d, k], recv_sem=recv_sem.at[phase, d, k],
            device_id={"dp": (right, left)[d]}, device_id_type=MESH)

    def arrive(phase, d, k):
        if phase < PD:
            bulk(phase, d, k).wait_recv()
            return
        h = 1 - d if phase == PX else d
        q = (left, right)[d] if phase != PE else opp
        ref = full.at[q, at(h, k)]
        pltpu.make_async_remote_copy(
            src_ref=ref, dst_ref=ref, send_sem=send_sem.at[phase, d, k], recv_sem=recv_sem.at[phase, d, k],
            device_id={"dp": (right, left)[d]}, device_id_type=MESH).wait_recv()

    loads[2].wait()
    for k in range(CHUNKS):
        for d in range(2):
            s_opp[at(d, k)] = own[2, at(d, k)].astype(f32)
    pl.semaphore_wait(barrier, count)
    for k in range(CHUNKS):
        for d in range(2):
            bulk(PA, d, k).start()
    loads[1].wait()
    loads[3].wait()
    for k in range(CHUNKS):
        for d, (dst, slot) in enumerate(((s_right, 1), (s_left, 3))):
            dst[at(1 - d, k)] = own[slot, at(1 - d, k)].astype(f32)
            bulk(PB, d, k).start()
    for copy in wloads:
        copy.wait()

    def weight_step(i, acc):
        w = held[y, pl.ds(pl.multiple_of(i * 8, 8), 8)]
        sq = w * w
        for j in range(width // 128):
            acc = acc + sq[:, j * 128:(j + 1) * 128]
        return acc

    w_lanes = lax.fori_loop(0, rows // 8, weight_step, jnp.zeros((8, 128), f32))
    for k in range(CHUNKS):
        for d, (dst, slot) in enumerate(((s_right, 1), (s_left, 3))):
            arrive(PA, d, k)
            dst[at(d, k)] = r_opp[at(d, k)] + own[slot, at(d, k)].astype(f32)
            bulk(PC, d, k).start()
    loads[0].wait()
    col_acc = jnp.zeros((8, width), f32)
    for k in range(CHUNKS):
        for d in range(2):
            arrive(PB, 1 - d, k)
            arrive(PC, d, k)
            g = own[0, at(d, k)].astype(f32) + r_left[at(d, k)] + r_right[at(d, k)]
            full[y, at(d, k)] = g
            bulk(PD, d, k).start()
            bulk(PX, 1 - d, k).start()
            sq = g * g
            for i in range(step // 8):
                col_acc = col_acc + sq[i * 8:(i + 1) * 8]
            part = sq[:, :128]
            for j in range(1, width // 128):
                part = part + sq[:, j * 128:(j + 1) * 128]
            lanes[at(d, k)] = part

    def send_small(stage, group, parts, own_slot):
        copies = []
        for d, dev, _ in peers(group):
            copies.append(pltpu.make_async_remote_copy(
                src_ref=parts.at[own_slot], dst_ref=parts.at[own_slot], send_sem=xs_sem.at[stage, d - 1],
                recv_sem=xr_sem.at[stage, d - 1], device_id=dev, device_id_type=MESH))
            copies[-1].start()
        return copies

    def wait_small(stage, group, parts):
        for d, dev, sender in peers(group):
            pltpu.make_async_remote_copy(
                src_ref=parts.at[sender], dst_ref=parts.at[sender], send_sem=xs_sem.at[stage, d - 1],
                recv_sem=xr_sem.at[stage, d - 1], device_id=dev, device_id_type=MESH).wait_recv()

    def total(parts, size):
        out = parts[0]
        for i in range(1, size):
            out = out + parts[i]
        return out

    pending = []
    stage = 0
    col_parts[r] = jnp.sum(col_acc, axis=0, keepdims=True)
    pending += send_small(stage, row_group, col_parts, r)
    value = jnp.sum(lanes[...].T, axis=0, keepdims=True)
    forwards = [(k, d) for k in range(CHUNKS) for d in range(2)]

    def forward(n):
        for _ in range(n):
            if forwards:
                k, d = forwards.pop(0)
                arrive(PD, d, k)
                bulk(PE, d, k).start()

    row_stages = []
    for i, group in enumerate(groups):
        stage += 1
        parts = row_parts.at[i]
        parts[group[1]] = value
        pending += send_small(stage, group, parts, group[1])
        if i == 0:
            wait_small(0, row_group, col_parts)
            load_col.wait()
            span = pl.ds(pl.multiple_of(y * width, 128), width)
            col_old[...] = colm[...].reshape(col_old.shape)
            mine = decay_rate * col_old[:, span] + (1.0 - decay_rate) * (total(col_parts, n_row) / rows_all + eps_one)
            col_all[:, span] = mine
            for d, dev, _ in peers(groups[0]):
                copy = pltpu.make_async_remote_copy(
                    src_ref=col_all.at[:, span], dst_ref=col_all.at[:, span], send_sem=cs_sem.at[d - 1],
                    recv_sem=cr_sem.at[d - 1], device_id=dev, device_id_type=MESH)
                copy.start()
                pending.append(copy)
            inverse = 1.0 / mine

            def raw_step(k, _):
                at_k = pl.ds(pl.multiple_of(k * 8, 8), 8)
                g = full[y, at_k]
                sq = g * g * inverse
                part = sq[:, :128]
                for j in range(1, width // 128):
                    part = part + sq[:, j * 128:(j + 1) * 128]
                lanes[at_k] = part
                return 0

            lax.fori_loop(0, rows // 8, raw_step, 0)
            raw_cols = jnp.sum(lanes[...].T, axis=0, keepdims=True)
        forward(1)
        wait_small(stage, group, parts)
        value = total(parts, group[2])
    load_row.wait()
    mine = decay_rate * rowm[...].reshape(1, rows) + (1.0 - decay_rate) * (value / cols_all + eps_one)
    row_new[...] = mine
    tile = jnp.concatenate([
        raw_cols / mine,
        mine * (1.0 / (n_dp * n_col)),
        jnp.sum(w_lanes, axis=0, keepdims=True),
        jnp.zeros((5, 128), f32)], axis=0)
    for i, group in enumerate(groups + [row_group]):
        stage += 1
        parts = scal_parts.at[i]
        parts[group[1]] = tile
        pending += send_small(stage, group, parts, group[1])
        forward(2)
        wait_small(stage, group, parts)
        tile = total(parts, group[2])
    forward(len(forwards))
    sums = jnp.sum(tile, axis=1, keepdims=True)
    row_mean = sums[1:2] / rows_all
    clip = jnp.maximum(1.0, jnp.sqrt(sums[0:1] * row_mean / entries) / clip_level)
    size = learn_rate * jnp.maximum(eps_two, jnp.sqrt(sums[2:3] / entries))
    scal[...] = jnp.concatenate([jnp.broadcast_to(clip, (1, 128)), jnp.broadcast_to(size, (1, 128))], axis=0)
    scale = lax.rsqrt(mine) * (jnp.sqrt(row_mean) / clip)
    row_scale[...] = jnp.broadcast_to(scale, (128, 128)).T
    for d, dev, sender in peers(groups[0]):
        ref = col_all.at[:, pl.ds(pl.multiple_of(sender * width, 128), width)]
        pltpu.make_async_remote_copy(
            src_ref=ref, dst_ref=ref, send_sem=cs_sem.at[d - 1], recv_sem=cr_sem.at[d - 1],
            device_id=dev, device_id_type=MESH).wait_recv()
    col_scale[...] = lax.rsqrt(col_all[...])
    for k in range(CHUNKS):
        for d in range(2):
            arrive(PX, d, k)
            arrive(PE, d, k)
    for copy in pending:
        copy.wait_send()
    for phase in range(6):
        for k in range(CHUNKS):
            for d in range(2):
                bulk(phase, d, k).wait_send()


def update_kernel(full, held, col_all, row_new, row_scale, col_scale, scal,
                  weight_out, update_out, row_out, col_out, clip_out,
                  new_weight, update, sem):
    rows, width = full.shape[1], full.shape[2]
    size = scal[1:2, :]
    step = 32
    copies = []
    for q in range(4):
        for k in range(rows // step):
            for i in range(step // 8):
                at = pl.ds(k * step + i * 8, 8)
                by_row = row_scale[at]
                for j in range(width // 128):
                    col = pl.ds(j * 128, 128)
                    u = full[q, at, col] * by_row * col_scale[:, pl.ds(q * width + j * 128, 128)]
                    update[q, at, col] = u
                    new_weight[q, at, col] = held[q, at, col] - size * u
            at = pl.ds(k * step, step)
            for which, (src, dst) in enumerate(((update, update_out), (new_weight, weight_out))):
                copies.append(pltpu.make_async_copy(
                    src.at[q, at], dst.at[at, pl.ds(q * width, width)], sem.at[which, q, k]))
                copies[-1].start()
    row_out[...] = row_new[...].reshape(row_out.shape)
    col_out[...] = col_all[...].reshape(col_out.shape)
    clip_out[...] = scal[0:1, 0:1]
    for copy in copies:
        copy.wait()


def solution(mesh):
    n_dp, n_row, n_col = mesh.shape["dp"], mesh.shape["row"], mesh.shape["col"]
    splits = ((4, 4), (4, 1)) if n_col == 16 else ((n_col, 1),)
    sizes = (n_dp, n_row, n_col, splits)

    def body(weight, grad_parts, row_moment, col_moment):
        rows, cols = weight.shape
        width = cols // n_dp
        vmem = pl.BlockSpec(memory_space=pltpu.VMEM)
        hbm = pl.BlockSpec(memory_space=pltpu.HBM)
        shapes = ((4, rows, width), (4, rows, width), (1, cols), (1, rows), (rows, 128), (1, cols), (2, 128))
        n_groups = 2 + len(splits)
        most = max(n_dp, n_row, *(s for s, _ in splits))
        stages = 1 + (n_groups - 1) + n_groups
        outs = pl.pallas_call(
            functools.partial(exchange_kernel, sizes),
            out_shape=tuple(pltpu.VMEM(s, f32) for s in shapes),
            in_specs=[hbm] * 4,
            out_specs=(vmem,) * len(shapes),
            scratch_shapes=[
                pltpu.VMEM((4, rows, width), jnp.bfloat16),
                *[pltpu.VMEM((rows, width), f32) for _ in range(6)],
                pltpu.VMEM((rows, 128), f32),
                pltpu.VMEM((rows,), f32),
                pltpu.VMEM((cols,), f32),
                pltpu.VMEM((1, cols), f32),
                pltpu.VMEM((n_row, 1, width), f32),
                pltpu.VMEM((n_groups - 1, most, 1, rows), f32),
                pltpu.VMEM((n_groups, most, 8, 128), f32),
                pltpu.SemaphoreType.DMA((10,)),
                pltpu.SemaphoreType.DMA((6, 2, CHUNKS)),
                pltpu.SemaphoreType.DMA((6, 2, CHUNKS)),
                pltpu.SemaphoreType.DMA((stages, most - 1)),
                pltpu.SemaphoreType.DMA((stages, most - 1)),
                pltpu.SemaphoreType.DMA((3,)),
                pltpu.SemaphoreType.DMA((3,)),
            ],
            compiler_params=pltpu.CompilerParams(
                collective_id=0, has_side_effects=True, vmem_limit_bytes=24 << 20),
            name="exchange",
        )(*(pltpu.with_memory_space_constraint(a, pltpu.HBM) for a in (grad_parts, weight, row_moment, col_moment)))
        new_weight, update, row_new, col_new, clip = pl.pallas_call(
            update_kernel,
            out_shape=(
                jax.ShapeDtypeStruct((rows, cols), f32),
                jax.ShapeDtypeStruct((rows, cols), f32),
                jax.ShapeDtypeStruct((rows,), f32),
                jax.ShapeDtypeStruct((cols,), f32),
                jax.ShapeDtypeStruct((1, 1), f32),
            ),
            in_specs=[vmem] * len(shapes),
            out_specs=(pl.BlockSpec(memory_space=pl.ANY), pl.BlockSpec(memory_space=pl.ANY), vmem, vmem, vmem),
            scratch_shapes=[
                pltpu.VMEM((4, rows, width), f32),
                pltpu.VMEM((4, rows, width), f32),
                pltpu.SemaphoreType.DMA((2, 4, rows // 32)),
            ],
            compiler_params=pltpu.CompilerParams(vmem_limit_bytes=24 << 20),
            name="apply",
        )(*outs)
        return new_weight, update, row_new, col_new, clip.reshape(())

    return jax.shard_map(
        body,
        mesh=mesh,
        in_specs=(P("row", "col"), P("dp", "row", "col"), P("row"), P("col")),
        out_specs=(P("row", "col"), P("row", "col"), P("row"), P("col"), P()),
        check_vma=False,
    )
```

time: 310 us -> 71.6 us (0.23)
  the two profiles are of different devices: /device:TPU:32 before, /device:TPU:1 now
where the time goes in v1:
time: 71.6 us; the launch traced here: 71.5 us
  Pallas kernels  70.9 us (99%)
    pallas_call x1, Pallas kernels, body(): pl.pallas_call(functools.partial(exchange_kernel, sizes), out_shape=tuple...  67.8 us
    pallas_call x1, Pallas kernels, body(): pl.pallas_call(update_kernel, out_shape=(jax.ShapeDtypeStruct((rows, cols...  3.06 us

profile of v1, /device:TPU:1, one launch (start us, length us, event | category | flops | bytes accessed | tf_op | source)
XLA Modules:
  0.0 71.5 jit_solution(4750597332419624479)
XLA Ops:
  0.6 67.8 %exchange.1 = (f32[4,128,1152]{2,1,0:T(8,128)S(1)}, f32[4,128,1152]{2,1,0:T(8,128)S(1)}, f32[1,4608]{1,0:T(1,128)S(1)}, f32[1,128]{1,0:T(1,128)S(1)}, f32[128,12...) custom-call(bf16[1,128,4608]{2,1,0:T(8,128)(2,1)} %grad_hbm.1, f32[128,4608]{1,0:T(8,128)} %weight_hbm.1, ...), custom_call_target="tpu_custom_call" | custom-call | tf_op jit(solution)/shard_map/exchange/pallas_call | solution.py:301
  68.5 3.1 %apply.1 = (f32[128,4608]{1,0:T(8,128)}, f32[128,4608]{1,0:T(8,128)}, f32[128]{0:T(128)}, f32[4608]{0:T(1024)}, f32[1,1]{1,0:T(1,128)}) custom-call(f32[4,128,1152]{2,1,0:T(8,128)S(1)} %get-tuple-element.17.full, f32[4,128,1152]{2,1,0:T(8,128)S(1)} %get-tuple-element.18.held, f32[1,4608]{1,0:T(1,128)S(1)} %get-tuple-element.19.col_all, ...), custom_call_target="tpu_custom_call" | custom-call | tf_op jit(solution)/shard_map/apply/pallas_call | solution.py:328

commit v2 on v1

v2 whole, which is shorter than its diff:
```python
import functools

import jax
import jax.numpy as jnp
from jax import lax
from jax.experimental import pallas as pl
from jax.experimental.pallas import tpu as pltpu
from jax.sharding import PartitionSpec as P

decay_rate = 0.5
eps_one = 1e-30
eps_two = 0.001
learn_rate = 0.01
clip_level = 1.0

MESH = pl.DeviceIdType.MESH
f32 = jnp.float32
CHUNKS = 4
PA, PB, PC, PD, PX, PE = range(6)


def exchange_kernel(sizes, grad_hbm, weight_hbm, rowm_hbm, colm_hbm,
                    full, held, col_all, row_new, row_scale, col_scale, scal,
                    own, s_opp, s_right, s_left, r_opp, r_left, r_right, lanes,
                    rowm, colm, col_old, col_parts, sums_col, sums_dp, sums_row,
                    load_sem, send_sem, recv_sem, xs_sem, xr_sem):
    n_dp, n_row, n_col = sizes
    rows, width = own.shape[1], own.shape[2]
    half = rows // 2
    step = half // CHUNKS
    rows_all = rows * n_row
    cols_all = width * n_dp * n_col
    entries = float(rows_all) * float(cols_all)
    y, r, c = lax.axis_index("dp"), lax.axis_index("row"), lax.axis_index("col")
    right, opp, left = lax.rem(y + 1, 4), lax.rem(y + 2, 4), lax.rem(y + 3, 4)

    dp_group, row_group, col_group = ("dp", y, n_dp), ("row", r, n_row), ("col", c, n_col)

    def peers(group):
        axis, at, size = group
        return [{axis: lax.rem(at + d, size)} for d in range(1, size)]

    loads = {}
    for slot, q in ((2, opp), (1, right), (3, left), (0, y)):
        loads[slot] = pltpu.make_async_copy(
            grad_hbm.at[0, :, pl.ds(pl.multiple_of(q * width, 128), width)], own.at[slot], load_sem.at[slot])
        loads[slot].start()
    barrier = pltpu.get_barrier_semaphore()
    count = 0
    for group in (dp_group, row_group, col_group):
        for dev in peers(group):
            pl.semaphore_signal(barrier, inc=1, device_id=dev, device_id_type=MESH)
            count += 1
    wloads = []
    for q in range(4):
        wloads.append(pltpu.make_async_copy(
            weight_hbm.at[:, pl.ds(q * width, width)], held.at[q], load_sem.at[4 + q]))
        wloads[-1].start()
    load_row = pltpu.make_async_copy(rowm_hbm, rowm, load_sem.at[8])
    load_col = pltpu.make_async_copy(colm_hbm, colm, load_sem.at[9])
    load_row.start()
    load_col.start()

    def at(h, k):
        return pl.ds(h * half + k * step, step)

    def bulk(phase, d, k):
        if phase == PA:
            src, dst = s_opp.at[at(d, k)], r_opp.at[at(d, k)]
        elif phase in (PB, PC):
            h = d if phase == PC else 1 - d
            src, dst = ((s_right, r_left), (s_left, r_right))[d]
            src, dst = src.at[at(h, k)], dst.at[at(h, k)]
        else:
            h = 1 - d if phase == PX else d
            q = y if phase != PE else (left, right)[d]
            src = dst = full.at[q, at(h, k)]
        return pltpu.make_async_remote_copy(
            src_ref=src, dst_ref=dst, send_sem=send_sem.at[phase, d, k], recv_sem=recv_sem.at[phase, d, k],
            device_id={"dp": (right, left)[d]}, device_id_type=MESH)

    def arrive(phase, d, k):
        if phase < PD:
            bulk(phase, d, k).wait_recv()
            return
        h = 1 - d if phase == PX else d
        q = (left, right)[d] if phase != PE else opp
        ref = full.at[q, at(h, k)]
        pltpu.make_async_remote_copy(
            src_ref=ref, dst_ref=ref, send_sem=send_sem.at[phase, d, k], recv_sem=recv_sem.at[phase, d, k],
            device_id={"dp": (right, left)[d]}, device_id_type=MESH).wait_recv()

    loads[2].wait()
    for k in range(CHUNKS):
        for d in range(2):
            s_opp[at(d, k)] = own[2, at(d, k)].astype(f32)
    pl.semaphore_wait(barrier, count)
    for k in range(CHUNKS):
        for d in range(2):
            bulk(PA, d, k).start()
    loads[1].wait()
    loads[3].wait()
    for k in range(CHUNKS):
        for d, (dst, slot) in enumerate(((s_right, 1), (s_left, 3))):
            dst[at(1 - d, k)] = own[slot, at(1 - d, k)].astype(f32)
            bulk(PB, d, k).start()
    for copy in wloads:
        copy.wait()

    def weight_step(i, acc):
        w = held[y, pl.ds(pl.multiple_of(i * 8, 8), 8)]
        sq = w * w
        for j in range(width // 128):
            acc = acc + sq[:, j * 128:(j + 1) * 128]
        return acc

    w_lanes = lax.fori_loop(0, rows // 8, weight_step, jnp.zeros((8, 128), f32))
    for k in range(CHUNKS):
        for d, (dst, slot) in enumerate(((s_right, 1), (s_left, 3))):
            arrive(PA, d, k)
            dst[at(d, k)] = r_opp[at(d, k)] + own[slot, at(d, k)].astype(f32)
            bulk(PC, d, k).start()
    loads[0].wait()
    col_acc = jnp.zeros((8, width), f32)
    for k in range(CHUNKS):
        for d in range(2):
            arrive(PB, 1 - d, k)
            arrive(PC, d, k)
            g = own[0, at(d, k)].astype(f32) + r_left[at(d, k)] + r_right[at(d, k)]
            full[y, at(d, k)] = g
            bulk(PD, d, k).start()
            bulk(PX, 1 - d, k).start()
            sq = g * g
            for i in range(step // 8):
                col_acc = col_acc + sq[i * 8:(i + 1) * 8]
            part = sq[:, :128]
            for j in range(1, width // 128):
                part = part + sq[:, j * 128:(j + 1) * 128]
            lanes[at(d, k)] = part

    def send_small(stage, group, parts):
        mine = parts.at[group[1]]
        copies = []
        for dev in peers(group):
            copies.append(pltpu.make_async_remote_copy(
                src_ref=mine, dst_ref=mine, send_sem=xs_sem.at[stage], recv_sem=xr_sem.at[stage],
                device_id=dev, device_id_type=MESH))
            copies[-1].start()

    def all_but_one(stage, group, parts):
        rest = parts.at[pl.ds(0, group[2] - 1)]
        return pltpu.make_async_remote_copy(
            src_ref=rest, dst_ref=rest, send_sem=xs_sem.at[stage], recv_sem=xr_sem.at[stage],
            device_id=peers(group)[0], device_id_type=MESH)

    def total(parts):
        out = parts[0]
        for i in range(1, parts.shape[0]):
            out = out + parts[i]
        return out

    col_parts[r] = jnp.sum(col_acc, axis=0, keepdims=True)
    send_small(0, row_group, col_parts)
    row_sums = jnp.sum(lanes[...].T, axis=0, keepdims=True)
    weight_sums = jnp.sum(w_lanes, axis=0, keepdims=True)
    load_col.wait()
    col_old[...] = colm[...].reshape(col_old.shape)
    span = pl.ds(pl.multiple_of(y * width, 128), width)
    old = col_old[:, span]
    all_but_one(0, row_group, col_parts).wait_recv()
    col_mine = decay_rate * old + (1.0 - decay_rate) * (total(col_parts) / rows_all + eps_one)
    inverse = 1.0 / col_mine

    def raw_step(k, _):
        at_k = pl.ds(pl.multiple_of(k * 8, 8), 8)
        g = full[y, at_k]
        sq = g * g * inverse
        part = sq[:, :128]
        for j in range(1, width // 128):
            part = part + sq[:, j * 128:(j + 1) * 128]
        lanes[at_k] = part
        return 0

    lax.fori_loop(0, rows // 8, raw_step, 0, unroll=4)
    raw_sums = jnp.sum(lanes[...].T, axis=0, keepdims=True)
    sums_col[c] = jnp.concatenate([row_sums, raw_sums, weight_sums, jnp.zeros((5, 128), f32)], axis=0)
    send_small(1, col_group, sums_col)
    col_all[:, span] = col_mine
    for dev in peers(dp_group):
        pltpu.make_async_remote_copy(
            src_ref=col_all.at[:, span], dst_ref=col_all.at[:, span], send_sem=xs_sem.at[4],
            recv_sem=xr_sem.at[4], device_id=dev, device_id_type=MESH).start()
    load_row.wait()
    all_but_one(1, col_group, sums_col).wait_recv()
    sums_dp[y] = total(sums_col)
    send_small(2, dp_group, sums_dp)
    for k in range(CHUNKS):
        for d in range(2):
            arrive(PD, d, k)
            bulk(PE, d, k).start()
    all_but_one(2, dp_group, sums_dp).wait_recv()
    tile = total(sums_dp)
    row_mine = decay_rate * rowm[...].reshape(1, rows) + (1.0 - decay_rate) * (tile[0:1] / cols_all + eps_one)
    row_new[...] = row_mine
    sums_row[r] = jnp.concatenate([tile[1:2] / row_mine, row_mine, tile[2:3], jnp.zeros((5, 128), f32)], axis=0)
    send_small(3, row_group, sums_row)
    cols_rest = col_all.at[:, pl.ds(0, 3 * width)]
    col_round = pltpu.make_async_remote_copy(
        src_ref=cols_rest, dst_ref=cols_rest, send_sem=xs_sem.at[4], recv_sem=xr_sem.at[4],
        device_id=peers(dp_group)[0], device_id_type=MESH)
    col_round.wait_recv()
    col_scale[...] = lax.rsqrt(col_all[...])
    all_but_one(3, row_group, sums_row).wait_recv()
    sums = jnp.sum(total(sums_row), axis=1, keepdims=True)
    row_mean = sums[1:2] / rows_all
    clip = jnp.maximum(1.0, jnp.sqrt(sums[0:1] * row_mean / entries) / clip_level)
    size = learn_rate * jnp.maximum(eps_two, jnp.sqrt(sums[2:3] / entries))
    scal[...] = jnp.concatenate([jnp.broadcast_to(clip, (1, 128)), jnp.broadcast_to(size, (1, 128))], axis=0)
    scale = lax.rsqrt(row_mine) * (jnp.sqrt(row_mean) / clip)
    row_scale[...] = jnp.broadcast_to(scale, (128, 128)).T
    for k in range(CHUNKS):
        for d in range(2):
            arrive(PX, d, k)
            arrive(PE, d, k)
    for stage, (group, parts) in enumerate(
            ((row_group, col_parts), (col_group, sums_col), (dp_group, sums_dp), (row_group, sums_row))):
        all_but_one(stage, group, parts).wait_send()
    col_round.wait_send()
    for phase in range(6):
        for k in range(CHUNKS):
            for d in range(2):
                bulk(phase, d, k).wait_send()


def update_kernel(full, held, col_all, row_new, row_scale, col_scale, scal,
                  weight_out, update_out, row_out, col_out, clip_out,
                  new_weight, update, sem):
    rows, width = full.shape[1], full.shape[2]
    size = scal[1:2, :]
    step = 16
    copies = []
    for k in range(rows // step):
        for i in range(step // 8):
            at = pl.ds(k * step + i * 8, 8)
            by_row = row_scale[at]
            for q in range(4):
                for j in range(width // 128):
                    col = pl.ds(j * 128, 128)
                    out = pl.ds(q * width + j * 128, 128)
                    u = full[q, at, col] * by_row * col_scale[:, out]
                    update[at, out] = u
                    new_weight[at, out] = held[q, at, col] - size * u
        at = pl.ds(k * step, step)
        for which, (src, dst) in enumerate(((update, update_out), (new_weight, weight_out))):
            copies.append(pltpu.make_async_copy(src.at[at], dst.at[at], sem.at[which, k]))
            copies[-1].start()
    row_out[...] = row_new[...].reshape(row_out.shape)
    col_out[...] = col_all[...].reshape(col_out.shape)
    clip_out[...] = scal[0:1, 0:1]
    for copy in copies:
        copy.wait()


def solution(mesh):
    n_dp, n_row, n_col = mesh.shape["dp"], mesh.shape["row"], mesh.shape["col"]
    sizes = (n_dp, n_row, n_col)

    def body(weight, grad_parts, row_moment, col_moment):
        rows, cols = weight.shape
        width = cols // n_dp
        vmem = pl.BlockSpec(memory_space=pltpu.VMEM)
        hbm = pl.BlockSpec(memory_space=pltpu.HBM)
        shapes = ((4, rows, width), (4, rows, width), (1, cols), (1, rows), (rows, 128), (1, cols), (2, 128))
        outs = pl.pallas_call(
            functools.partial(exchange_kernel, sizes),
            out_shape=tuple(pltpu.VMEM(s, f32) for s in shapes),
            in_specs=[hbm] * 4,
            out_specs=(vmem,) * len(shapes),
            scratch_shapes=[
                pltpu.VMEM((4, rows, width), jnp.bfloat16),
                *[pltpu.VMEM((rows, width), f32) for _ in range(6)],
                pltpu.VMEM((rows, 128), f32),
                pltpu.VMEM((rows,), f32),
                pltpu.VMEM((cols,), f32),
                pltpu.VMEM((1, cols), f32),
                pltpu.VMEM((n_row, 1, width), f32),
                pltpu.VMEM((n_col, 8, 128), f32),
                pltpu.VMEM((n_dp, 8, 128), f32),
                pltpu.VMEM((n_row, 8, 128), f32),
                pltpu.SemaphoreType.DMA((10,)),
                pltpu.SemaphoreType.DMA((6, 2, CHUNKS)),
                pltpu.SemaphoreType.DMA((6, 2, CHUNKS)),
                pltpu.SemaphoreType.DMA((5,)),
                pltpu.SemaphoreType.DMA((5,)),
            ],
            compiler_params=pltpu.CompilerParams(
                collective_id=0, has_side_effects=True, vmem_limit_bytes=24 << 20),
            name="exchange",
        )(*(pltpu.with_memory_space_constraint(a, pltpu.HBM) for a in (grad_parts, weight, row_moment, col_moment)))
        new_weight, update, row_new, col_new, clip = pl.pallas_call(
            update_kernel,
            out_shape=(
                jax.ShapeDtypeStruct((rows, cols), f32),
                jax.ShapeDtypeStruct((rows, cols), f32),
                jax.ShapeDtypeStruct((rows,), f32),
                jax.ShapeDtypeStruct((cols,), f32),
                jax.ShapeDtypeStruct((1, 1), f32),
            ),
            in_specs=[vmem] * len(shapes),
            out_specs=(pl.BlockSpec(memory_space=pl.ANY), pl.BlockSpec(memory_space=pl.ANY), vmem, vmem, vmem),
            scratch_shapes=[
                pltpu.VMEM((rows, cols), f32),
                pltpu.VMEM((rows, cols), f32),
                pltpu.SemaphoreType.DMA((2, rows // 16)),
            ],
            compiler_params=pltpu.CompilerParams(vmem_limit_bytes=24 << 20),
            name="apply",
        )(*outs)
        return new_weight, update, row_new, col_new, clip.reshape(())

    return jax.shard_map(
        body,
        mesh=mesh,
        in_specs=(P("row", "col"), P("dp", "row", "col"), P("row"), P("col")),
        out_specs=(P("row", "col"), P("row", "col"), P("row"), P("col"), P()),
        check_vma=False,
    )
```

time: 71.6 us -> 56.4 us (0.79)
  Pallas kernels: 70.9 us -> 55.7 us
    pallas_call x1, Pallas kernels: 67.8 us -> 52.7 us  [body(): pl.pallas_call(functools.partial(exchange_kernel, sizes), out_shape=tuple...]
where the time goes in v2:
time: 56.4 us; the launch traced here: 56.3 us
  Pallas kernels  55.7 us (99%)
  between operations  0.64 us (1%)
    pallas_call x1, Pallas kernels, body(): pl.pallas_call(functools.partial(exchange_kernel, sizes), out_shape=tuple...  52.7 us
    pallas_call x1, Pallas kernels, body(): pl.pallas_call(update_kernel, out_shape=(jax.ShapeDtypeStruct((rows, cols...  2.95 us

profile of v2, /device:TPU:1, one launch (start us, length us, event | category | flops | bytes accessed | tf_op | source)
XLA Modules:
  0.0 56.3 jit_solution(12732114979717346053)
XLA Ops:
  0.6 52.7 %exchange.1 = (f32[4,128,1152]{2,1,0:T(8,128)S(1)}, f32[4,128,1152]{2,1,0:T(8,128)S(1)}, f32[1,4608]{1,0:T(1,128)S(1)}, f32[1,128]{1,0:T(1,128)S(1)}, f32[128,12...) custom-call(bf16[1,128,4608]{2,1,0:T(8,128)(2,1)} %grad_hbm.1, f32[128,4608]{1,0:T(8,128)} %weight_hbm.1, ...), custom_call_target="tpu_custom_call" | custom-call | tf_op jit(solution)/shard_map/exchange/pallas_call | solution.py:274
  53.4 3.0 %apply.1 = (f32[128,4608]{1,0:T(8,128)}, f32[128,4608]{1,0:T(8,128)}, f32[128]{0:T(128)}, f32[4608]{0:T(1024)}, f32[1,1]{1,0:T(1,128)}) custom-call(f32[4,128,1152]{2,1,0:T(8,128)S(1)} %get-tuple-element.17.full, f32[4,128,1152]{2,1,0:T(8,128)S(1)} %get-tuple-element.18.held, f32[1,4608]{1,0:T(1,128)S(1)} %get-tuple-element.19.col_all, ...), custom_call_target="tpu_custom_call" | custom-call | tf_op jit(solution)/shard_map/apply/pallas_call | solution.py:300

commit v3 on v2

--- a/solution.py
+++ b/solution.py
@@ -23,7 +23,7 @@
                     full, held, col_all, row_new, row_scale, col_scale, scal,
                     own, s_opp, s_right, s_left, r_opp, r_left, r_right, lanes,
                     rowm, colm, col_old, col_parts, sums_col, sums_dp, sums_row,
-                    load_sem, send_sem, recv_sem, xs_sem, xr_sem):
+                    load_sem, send_sem, recv_sem, xs_sem, xr_sem, ready):
     n_dp, n_row, n_col = sizes
     rows, width = own.shape[1], own.shape[2]
     half = rows // 2
@@ -44,22 +44,44 @@
     for slot, q in ((2, opp), (1, right), (3, left), (0, y)):
         loads[slot] = pltpu.make_async_copy(
             grad_hbm.at[0, :, pl.ds(pl.multiple_of(q * width, 128), width)], own.at[slot], load_sem.at[slot])
-        loads[slot].start()
+    for q in range(4):
+        loads[4 + q] = pltpu.make_async_copy(
+            weight_hbm.at[:, pl.ds(q * width, width)], held.at[q], load_sem.at[4 + q])
+    loads[8] = pltpu.make_async_copy(rowm_hbm, rowm, load_sem.at[8])
+    loads[9] = pltpu.make_async_copy(colm_hbm, colm, load_sem.at[9])
+    loads[2].start()
     barrier = pltpu.get_barrier_semaphore()
-    count = 0
-    for group in (dp_group, row_group, col_group):
-        for dev in peers(group):
-            pl.semaphore_signal(barrier, inc=1, device_id=dev, device_id_type=MESH)
-            count += 1
-    wloads = []
-    for q in range(4):
-        wloads.append(pltpu.make_async_copy(
-            weight_hbm.at[:, pl.ds(q * width, width)], held.at[q], load_sem.at[4 + q]))
-        wloads[-1].start()
-    load_row = pltpu.make_async_copy(rowm_hbm, rowm, load_sem.at[8])
-    load_col = pltpu.make_async_copy(colm_hbm, colm, load_sem.at[9])
-    load_row.start()
-    load_col.start()
+    place = lax.rem(c, 4) * (n_col // 4) + c // 4
+    for dev in peers(dp_group):
+        pl.semaphore_signal(barrier, inc=1, device_id=dev, device_id_type=MESH)
+    for d in range(1, n_col):
+        peer = lax.rem(c + d, n_col)
+
+        @pl.when(lax.rem(peer, 4) * (n_col // 4) + peer // 4 > place)
+        def _():
+            pl.semaphore_signal(barrier, inc=1, device_id={"col": peer}, device_id_type=MESH)
+
+    for d in range(1, n_row):
+        peer = lax.rem(r + d, n_row)
+
+        @pl.when(peer > r)
+        def _():
+            pl.semaphore_signal(barrier, inc=1, device_id={"row": peer}, device_id_type=MESH)
+
+    def answer():
+        for d in range(1, n_col):
+            peer = lax.rem(c + d, n_col)
+
+            @pl.when(lax.rem(peer, 4) * (n_col // 4) + peer // 4 < place)
+            def _():
+                pl.semaphore_signal(ready, inc=1, device_id={"col": peer}, device_id_type=MESH)
+
+        for d in range(1, n_row):
+            peer = lax.rem(r + d, n_row)
+
+            @pl.when(peer < r)
+            def _():
+                pl.semaphore_signal(ready, inc=1, device_id={"row": peer}, device_id_type=MESH)
 
     def at(h, k):
         return pl.ds(h * half + k * step, step)
@@ -94,18 +116,39 @@
     for k in range(CHUNKS):
         for d in range(2):
             s_opp[at(d, k)] = own[2, at(d, k)].astype(f32)
-    pl.semaphore_wait(barrier, count)
+    pl.semaphore_wait(barrier, n_dp - 1 + place + r)
     for k in range(CHUNKS):
         for d in range(2):
             bulk(PA, d, k).start()
+    for i in (1, 3, 0, 4, 5, 6, 7, 8, 9):
+        loads[i].start()
     loads[1].wait()
     loads[3].wait()
     for k in range(CHUNKS):
         for d, (dst, slot) in enumerate(((s_right, 1), (s_left, 3))):
             dst[at(1 - d, k)] = own[slot, at(1 - d, k)].astype(f32)
+    answer()
+
+    def first(k):
+        for d in range(2):
+            bulk(PA, d, k).wait_send()
             bulk(PB, d, k).start()
-    for copy in wloads:
-        copy.wait()
+
+    def second(k):
+        for d, (dst, slot) in enumerate(((s_right, 1), (s_left, 3))):
+            arrive(PA, d, k)
+            dst[at(d, k)] = r_opp[at(d, k)] + own[slot, at(d, k)].astype(f32)
+            bulk(PC, d, k).start()
+
+    first(0)
+    first(1)
+    for k in range(2, CHUNKS):
+        second(k - 2)
+        first(k)
+    second(CHUNKS - 2)
+    second(CHUNKS - 1)
+    for q in range(4):
+        loads[4 + q].wait()
 
     def weight_step(i, acc):
         w = held[y, pl.ds(pl.multiple_of(i * 8, 8), 8)]
@@ -115,11 +158,6 @@
         return acc
 
     w_lanes = lax.fori_loop(0, rows // 8, weight_step, jnp.zeros((8, 128), f32))
-    for k in range(CHUNKS):
-        for d, (dst, slot) in enumerate(((s_right, 1), (s_left, 3))):
-            arrive(PA, d, k)
-            dst[at(d, k)] = r_opp[at(d, k)] + own[slot, at(d, k)].astype(f32)
-            bulk(PC, d, k).start()
     loads[0].wait()
     col_acc = jnp.zeros((8, width), f32)
     for k in range(CHUNKS):
@@ -129,7 +167,6 @@
             g = own[0, at(d, k)].astype(f32) + r_left[at(d, k)] + r_right[at(d, k)]
             full[y, at(d, k)] = g
             bulk(PD, d, k).start()
-            bulk(PX, 1 - d, k).start()
             sq = g * g
             for i in range(step // 8):
                 col_acc = col_acc + sq[i * 8:(i + 1) * 8]
@@ -159,11 +196,29 @@
             out = out + parts[i]
         return out
 
+    def others(ks):
+        for k in ks:
+            for d in range(2):
+                bulk(PX, d, k).start()
+
+    def forward(ks):
+        for k in ks:
+            for d in range(2):
+                arrive(PD, d, k)
+                bulk(PE, d, k).start()
+
+    others(range(CHUNKS // 2))
+    later = n_col - 1 - place + n_row - 1 - r
+
+    @pl.when(later > 0)
+    def _():
+        pl.semaphore_wait(ready, later)
+
     col_parts[r] = jnp.sum(col_acc, axis=0, keepdims=True)
     send_small(0, row_group, col_parts)
     row_sums = jnp.sum(lanes[...].T, axis=0, keepdims=True)
     weight_sums = jnp.sum(w_lanes, axis=0, keepdims=True)
-    load_col.wait()
+    loads[9].wait()
     col_old[...] = colm[...].reshape(col_old.shape)
     span = pl.ds(pl.multiple_of(y * width, 128), width)
     old = col_old[:, span]
@@ -190,14 +245,13 @@
         pltpu.make_async_remote_copy(
             src_ref=col_all.at[:, span], dst_ref=col_all.at[:, span], send_sem=xs_sem.at[4],
             recv_sem=xr_sem.at[4], device_id=dev, device_id_type=MESH).start()
-    load_row.wait()
+    others(range(CHUNKS // 2, CHUNKS))
+    loads[8].wait()
+    forward(range(CHUNKS // 2))
     all_but_one(1, col_group, sums_col).wait_recv()
     sums_dp[y] = total(sums_col)
     send_small(2, dp_group, sums_dp)
-    for k in range(CHUNKS):
-        for d in range(2):
-            arrive(PD, d, k)
-            bulk(PE, d, k).start()
+    forward(range(CHUNKS // 2, CHUNKS))
     all_but_one(2, dp_group, sums_dp).wait_recv()
     tile = total(sums_dp)
     row_mine = decay_rate * rowm[...].reshape(1, rows) + (1.0 - decay_rate) * (tile[0:1] / cols_all + eps_one)
@@ -226,7 +280,7 @@
             ((row_group, col_parts), (col_group, sums_col), (dp_group, sums_dp), (row_group, sums_row))):
         all_but_one(stage, group, parts).wait_send()
     col_round.wait_send()
-    for phase in range(6):
+    for phase in (PB, PC, PD, PX, PE):
         for k in range(CHUNKS):
             for d in range(2):
                 bulk(phase, d, k).wait_send()
@@ -292,6 +346,7 @@
                 pltpu.SemaphoreType.DMA((6, 2, CHUNKS)),
                 pltpu.SemaphoreType.DMA((5,)),
                 pltpu.SemaphoreType.DMA((5,)),
+                pltpu.SemaphoreType.REGULAR,
             ],
             compiler_params=pltpu.CompilerParams(
                 collective_id=0, has_side_effects=True, vmem_limit_bytes=24 << 20),

time: 56.4 us -> 52.2 us (0.926)
  Pallas kernels: 55.7 us -> 51.4 us
    pallas_call x1, Pallas kernels: 52.7 us -> 48.4 us  [body(): pl.pallas_call(functools.partial(exchange_kernel, sizes), out_shape=tuple...]
where the time goes in v3:
time: 52.2 us; the launch traced here: 52 us
  Pallas kernels  51.4 us (98%)
  between operations  0.64 us (1%)
    pallas_call x1, Pallas kernels, body(): pl.pallas_call(functools.partial(exchange_kernel, sizes), out_shape=tuple...  48.4 us
    pallas_call x1, Pallas kernels, body(): pl.pallas_call(update_kernel, out_shape=(jax.ShapeDtypeStruct((rows, cols...  2.95 us

profile of v3, /device:TPU:1, one launch (start us, length us, event | category | flops | bytes accessed | tf_op | source)
XLA Modules:
  0.0 52.0 jit_solution(15668206432597167613)
XLA Ops:
  0.6 48.4 %exchange.1 = (f32[4,128,1152]{2,1,0:T(8,128)S(1)}, f32[4,128,1152]{2,1,0:T(8,128)S(1)}, f32[1,4608]{1,0:T(1,128)S(1)}, f32[1,128]{1,0:T(1,128)S(1)}, f32[128,12...) custom-call(bf16[1,128,4608]{2,1,0:T(8,128)(2,1)} %grad_hbm.1, f32[128,4608]{1,0:T(8,128)} %weight_hbm.1, ...), custom_call_target="tpu_custom_call" | custom-call | tf_op jit(solution)/shard_map/exchange/pallas_call | solution.py:328
  49.1 3.0 %apply.1 = (f32[128,4608]{1,0:T(8,128)}, f32[128,4608]{1,0:T(8,128)}, f32[128]{0:T(128)}, f32[4608]{0:T(1024)}, f32[1,1]{1,0:T(1,128)}) custom-call(f32[4,128,1152]{2,1,0:T(8,128)S(1)} %get-tuple-element.17.full, f32[4,128,1152]{2,1,0:T(8,128)S(1)} %get-tuple-element.18.held, f32[1,4608]{1,0:T(1,128)S(1)} %get-tuple-element.19.col_all, ...), custom_call_target="tpu_custom_call" | custom-call | tf_op jit(solution)/shard_map/apply/pallas_call | solution.py:355

commit v4 on v2

v4 whole, which is shorter than its diff:
```python
import functools

import jax
import jax.numpy as jnp
from jax import lax
from jax.experimental import pallas as pl
from jax.experimental.pallas import tpu as pltpu
from jax.sharding import PartitionSpec as P

decay_rate = 0.5
eps_one = 1e-30
eps_two = 0.001
learn_rate = 0.01
clip_level = 1.0

MESH = pl.DeviceIdType.MESH
f32 = jnp.float32
PA, PB, PC, PD, PX, PE = range(6)
PIECES = (4, 1, 4, 4, 1, 4)


def exchange_kernel(sizes, grad_hbm, weight_hbm, rowm_hbm, colm_hbm,
                    full, held, col_all, row_new, row_scale, col_scale, scal,
                    own, s_opp, s_right, s_left, r_opp, r_left, r_right, lanes,
                    rowm, colm, col_old, col_parts, sums_yx, sums_zr,
                    load_sem, send_sem, recv_sem, xs_sem, xr_sem, ready):
    rows_all, cols_all = sizes
    rows, width = own.shape[1], own.shape[2]
    half = rows // 2
    entries = float(rows_all) * float(cols_all)
    y, r, c = lax.axis_index("dp"), lax.axis_index("row"), lax.axis_index("col")
    x, z = c // 4, lax.rem(c, 4)
    right, opp, left = lax.rem(y + 1, 4), lax.rem(y + 2, 4), lax.rem(y + 3, 4)

    loads = {}
    for slot, q in ((2, opp), (1, right), (3, left), (0, y)):
        loads[slot] = pltpu.make_async_copy(
            grad_hbm.at[0, :, pl.ds(pl.multiple_of(q * width, 128), width)], own.at[slot], load_sem.at[slot])
    for q in range(4):
        loads[4 + q] = pltpu.make_async_copy(
            weight_hbm.at[:, pl.ds(q * width, width)], held.at[q], load_sem.at[4 + q])
    loads[8] = pltpu.make_async_copy(rowm_hbm, rowm, load_sem.at[8])
    loads[9] = pltpu.make_async_copy(colm_hbm, colm, load_sem.at[9])

    barrier = pltpu.get_barrier_semaphore()
    place = z * 4 + r

    def greet(sem, later):
        sign = 1 if later else -1
        for d in range(1, 4):
            for which, at in (("x", x), ("z", z), ("r", r)):
                to = at + sign * d

                @pl.when((to < 4) if later else (to >= 0))
                def _():
                    for i in range(4):
                        if which == "x":
                            dev = {"dp": i, "col": to * 4 + z}
                        elif which == "z":
                            dev = {"col": x * 4 + to, "row": i}
                        else:
                            dev = {"row": to}
                        if which != "r" or i == 0:
                            pl.semaphore_signal(sem, inc=1, device_id=dev, device_id_type=MESH)

    for q in (right, left, opp):
        pl.semaphore_signal(barrier, inc=1, device_id={"dp": q}, device_id_type=MESH)
    loads[2].start()
    greet(barrier, True)

    def at(phase, h, k):
        step = half // PIECES[phase]
        return pl.ds(h * half + k * step, step)

    def bulk(phase, d, k=0):
        if phase == PA:
            src, dst = s_opp.at[at(phase, d, k)], r_opp.at[at(phase, d, k)]
        elif phase in (PB, PC):
            h = d if phase == PC else 1 - d
            src, dst = ((s_right, r_left), (s_left, r_right))[d]
            src, dst = src.at[at(phase, h, k)], dst.at[at(phase, h, k)]
        else:
            h = 1 - d if phase == PX else d
            q = y if phase != PE else (left, right)[d]
            src = dst = full.at[q, at(phase, h, k)]
        return pltpu.make_async_remote_copy(
            src_ref=src, dst_ref=dst, send_sem=send_sem.at[phase, d, k], recv_sem=recv_sem.at[phase, d, k],
            device_id={"dp": (right, left)[d]}, device_id_type=MESH)

    def arrive(phase, d, k=0):
        if phase < PD:
            bulk(phase, d, k).wait_recv()
            return
        h = 1 - d if phase == PX else d
        q = (left, right)[d] if phase != PE else opp
        ref = full.at[q, at(phase, h, k)]
        pltpu.make_async_remote_copy(
            src_ref=ref, dst_ref=ref, send_sem=send_sem.at[phase, d, k], recv_sem=recv_sem.at[phase, d, k],
            device_id={"dp": (right, left)[d]}, device_id_type=MESH).wait_recv()

    def sent(phase):
        for k in range(PIECES[phase]):
            for d in range(2):
                bulk(phase, d, k).wait_send()

    loads[2].wait()
    s_opp[...] = own[2].astype(f32)
    pl.semaphore_wait(barrier, 3 + 4 * x + place)
    for k in range(PIECES[PA]):
        for d in range(2):
            bulk(PA, d, k).start()
    for i in (1, 3, 0, 4, 5, 6, 7, 8, 9):
        loads[i].start()
    loads[1].wait()
    loads[3].wait()
    for d, (dst, slot) in enumerate(((s_right, 1), (s_left, 3))):
        span = at(PB, 1 - d, 0)
        dst[span] = own[slot, span].astype(f32)
        bulk(PB, d).start()
    greet(ready, False)
    for i in (0, 4, 5, 6, 7, 8, 9):
        loads[i].wait()

    def weight_step(i, acc):
        w = held[y, pl.ds(pl.multiple_of(i * 8, 8), 8)]
        sq = w * w
        for j in range(width // 128):
            acc = acc + sq[:, j * 128:(j + 1) * 128]
        return acc

    w_lanes = lax.fori_loop(0, rows // 8, weight_step, jnp.zeros((8, 128), f32), unroll=2)
    weight_sums = jnp.sum(w_lanes, axis=0, keepdims=True)
    col_old[...] = colm[...].reshape(col_old.shape)
    mine = pl.ds(pl.multiple_of(y * width, 128), width)
    row_old = rowm[...].reshape(1, rows)
    for k in range(PIECES[PC]):
        for d, (dst, slot) in enumerate(((s_right, 1), (s_left, 3))):
            span = at(PC, d, k)
            arrive(PA, d, k)
            dst[span] = r_opp[span] + own[slot, span].astype(f32)
            bulk(PC, d, k).start()
    sent(PA)
    col_acc = jnp.zeros((8, width), f32)
    arrive(PB, 0)
    arrive(PB, 1)
    for k in range(PIECES[PC]):
        for d in range(2):
            span = at(PC, d, k)
            arrive(PC, d, k)
            g = own[0, span].astype(f32) + r_left[span] + r_right[span]
            full[y, span] = g
            bulk(PD, d, k).start()
            sq = g * g
            for i in range(sq.shape[0] // 8):
                col_acc = col_acc + sq[i * 8:(i + 1) * 8]
            part = sq[:, :128]
            for j in range(1, width // 128):
                part = part + sq[:, j * 128:(j + 1) * 128]
            lanes[span] = part

    def send_small(stage, parts, at, devs):
        ref = parts.at[at]
        for i, dev in devs:
            @pl.when(at != i)
            def _():
                pltpu.make_async_remote_copy(
                    src_ref=ref, dst_ref=ref, send_sem=xs_sem.at[stage], recv_sem=xr_sem.at[stage],
                    device_id=dev, device_id_type=MESH).start()

    def whole(stage, parts, dev):
        rest = parts.at[pl.ds(0, parts.shape[0] - 1)]
        return pltpu.make_async_remote_copy(
            src_ref=rest, dst_ref=rest, send_sem=xs_sem.at[stage], recv_sem=xr_sem.at[stage],
            device_id=dev, device_id_type=MESH)

    def total(parts):
        out = parts[0]
        for i in range(1, parts.shape[0]):
            out = out + parts[i]
        return out

    near = {"row": lax.rem(r + 1, 4)}
    later = 12 - 4 * x + 15 - place

    @pl.when(later > 0)
    def _():
        pl.semaphore_wait(ready, later)

    col_parts[r] = jnp.sum(col_acc, axis=0, keepdims=True)
    send_small(0, col_parts, r, [(i, {"row": i}) for i in range(4)])
    row_sums = jnp.sum(lanes[...].T, axis=0, keepdims=True)
    old = decay_rate * col_old[:, mine]
    whole(0, col_parts, near).wait_recv()
    col_mine = old + (1.0 - decay_rate) * (total(col_parts) / rows_all + eps_one)
    inverse = 1.0 / col_mine

    def raw_step(k, _):
        span = pl.ds(pl.multiple_of(k * 8, 8), 8)
        g = full[y, span]
        sq = g * g * inverse
        part = sq[:, :128]
        for j in range(1, width // 128):
            part = part + sq[:, j * 128:(j + 1) * 128]
        lanes[span] = part
        return 0

    lax.fori_loop(0, rows // 8, raw_step, 0, unroll=4)
    raw_sums = jnp.sum(lanes[...].T, axis=0, keepdims=True)
    sums_yx[y * 4 + x] = jnp.concatenate([row_sums, raw_sums, weight_sums, jnp.zeros((5, 128), f32)], axis=0)
    send_small(1, sums_yx, y * 4 + x, [(i * 4 + j, {"dp": i, "col": j * 4 + z}) for i in range(4) for j in range(4)])
    for d in range(2):
        bulk(PX, d).start()
    col_all[:, mine] = col_mine
    for q in (right, left, opp):
        pltpu.make_async_remote_copy(
            src_ref=col_all.at[:, mine], dst_ref=col_all.at[:, mine], send_sem=xs_sem.at[3],
            recv_sem=xr_sem.at[3], device_id={"dp": q}, device_id_type=MESH).start()
    for k in range(PIECES[PE]):
        for d in range(2):
            arrive(PD, d, k)
            bulk(PE, d, k).start()
    whole(1, sums_yx, {"dp": right}).wait_recv()
    sums_zr[place] = jnp.concatenate([total(sums_yx)[0:3], row_old, jnp.zeros((4, 128), f32)], axis=0)
    send_small(2, sums_zr, place, [(i * 4 + j, {"col": x * 4 + i, "row": j}) for i in range(4) for j in range(4)])
    cols_rest = col_all.at[:, pl.ds(0, 3 * width)]
    cols = pltpu.make_async_remote_copy(
        src_ref=cols_rest, dst_ref=cols_rest, send_sem=xs_sem.at[3], recv_sem=xr_sem.at[3],
        device_id={"dp": right}, device_id_type=MESH)
    cols.wait()
    col_scale[...] = lax.rsqrt(col_all[...])
    whole(0, col_parts, near).wait_send()
    whole(1, sums_yx, {"dp": right}).wait_send()
    for phase in (PB, PC, PD, PX, PE):
        sent(phase)
    for d in range(2):
        arrive(PX, d)
        for k in range(PIECES[PE]):
            arrive(PE, d, k)
    whole(2, sums_zr, near).wait_recv()

    def moments(group):
        tile = sums_zr[group]
        for i in range(1, 4):
            tile = tile + sums_zr[i * 4 + group]
        return tile, (decay_rate * 0.25) * tile[3:4] + (1.0 - decay_rate) * (tile[0:1] / cols_all + eps_one)

    _, row_mine = moments(r)
    row_new[...] = row_mine
    row_scale[...] = jnp.broadcast_to(lax.rsqrt(row_mine), (128, 128)).T
    sums = [jnp.zeros((1, 128), f32)] * 3
    for group in range(4):
        tile, row_one = moments(group)
        for i, part in enumerate((tile[1:2] / row_one, row_one, tile[2:3])):
            sums[i] = sums[i] + part
    sums = jnp.sum(jnp.concatenate(sums, axis=0), axis=1, keepdims=True)
    row_mean = sums[1:2] / rows_all
    clip = jnp.maximum(1.0, jnp.sqrt(sums[0:1] * row_mean / entries) / clip_level)
    size = learn_rate * jnp.maximum(eps_two, jnp.sqrt(sums[2:3] / entries))
    scal[...] = jnp.concatenate(
        [jnp.broadcast_to(v, (1, 128)) for v in (clip, size, jnp.sqrt(row_mean) / clip, clip)], axis=0)
    whole(2, sums_zr, near).wait_send()


def update_kernel(full, held, col_all, row_new, row_scale, col_scale, scal,
                  weight_out, update_out, row_out, col_out, clip_out,
                  new_weight, update, sem):
    rows, width = full.shape[1], full.shape[2]
    size, factor = scal[1:2, :], scal[2:3, :]
    step = 16
    copies = []
    for k in range(rows // step):
        for i in range(step // 8):
            at = pl.ds(k * step + i * 8, 8)
            by_row = row_scale[at] * factor
            for q in range(4):
                for j in range(width // 128):
                    col = pl.ds(j * 128, 128)
                    out = pl.ds(q * width + j * 128, 128)
                    u = full[q, at, col] * by_row * col_scale[:, out]
                    update[at, out] = u
                    new_weight[at, out] = held[q, at, col] - size * u
        at = pl.ds(k * step, step)
        for which, (src, dst) in enumerate(((update, update_out), (new_weight, weight_out))):
            copies.append(pltpu.make_async_copy(src.at[at], dst.at[at], sem.at[which, k]))
            copies[-1].start()
    row_out[...] = row_new[...].reshape(row_out.shape)
    col_out[...] = col_all[...].reshape(col_out.shape)
    clip_out[...] = scal[0:1, 0:1]
    for copy in copies:
        copy.wait()


def solution(mesh):
    assert all(mesh.shape[axis] == size for axis, size in (("dp", 4), ("row", 4), ("col", 16)))

    def body(weight, grad_parts, row_moment, col_moment):
        rows, cols = weight.shape
        width = cols // 4
        vmem = pl.BlockSpec(memory_space=pltpu.VMEM)
        hbm = pl.BlockSpec(memory_space=pltpu.HBM)
        shapes = ((4, rows, width), (4, rows, width), (1, cols), (1, rows), (rows, 128), (1, cols), (4, 128))
        outs = pl.pallas_call(
            functools.partial(exchange_kernel, (rows * 4, cols * 16)),
            out_shape=tuple(pltpu.VMEM(s, f32) for s in shapes),
            in_specs=[hbm] * 4,
            out_specs=(vmem,) * len(shapes),
            scratch_shapes=[
                pltpu.VMEM((4, rows, width), jnp.bfloat16),
                *[pltpu.VMEM((rows, width), f32) for _ in range(6)],
                pltpu.VMEM((rows, 128), f32),
                pltpu.VMEM((rows,), f32),
                pltpu.VMEM((cols,), f32),
                pltpu.VMEM((1, cols), f32),
                pltpu.VMEM((4, 1, width), f32),
                pltpu.VMEM((16, 8, 128), f32),
                pltpu.VMEM((16, 8, 128), f32),
                pltpu.SemaphoreType.DMA((10,)),
                pltpu.SemaphoreType.DMA((6, 2, max(PIECES))),
                pltpu.SemaphoreType.DMA((6, 2, max(PIECES))),
                pltpu.SemaphoreType.DMA((4,)),
                pltpu.SemaphoreType.DMA((4,)),
                pltpu.SemaphoreType.REGULAR,
            ],
            compiler_params=pltpu.CompilerParams(
                collective_id=0, has_side_effects=True, vmem_limit_bytes=24 << 20),
            name="exchange",
        )(*(pltpu.with_memory_space_constraint(a, pltpu.HBM) for a in (grad_parts, weight, row_moment, col_moment)))
        new_weight, update, row_new, col_new, clip = pl.pallas_call(
            update_kernel,
            out_shape=(
                jax.ShapeDtypeStruct((rows, cols), f32),
                jax.ShapeDtypeStruct((rows, cols), f32),
                jax.ShapeDtypeStruct((rows,), f32),
                jax.ShapeDtypeStruct((cols,), f32),
                jax.ShapeDtypeStruct((1, 1), f32),
            ),
            in_specs=[vmem] * len(shapes),
            out_specs=(pl.BlockSpec(memory_space=pl.ANY), pl.BlockSpec(memory_space=pl.ANY), vmem, vmem, vmem),
            scratch_shapes=[
                pltpu.VMEM((rows, cols), f32),
                pltpu.VMEM((rows, cols), f32),
                pltpu.SemaphoreType.DMA((2, rows // 16)),
            ],
            compiler_params=pltpu.CompilerParams(vmem_limit_bytes=24 << 20),
            name="apply",
        )(*outs)
        return new_weight, update, row_new, col_new, clip.reshape(())

    return jax.shard_map(
        body,
        mesh=mesh,
        in_specs=(P("row", "col"), P("dp", "row", "col"), P("row"), P("col")),
        out_specs=(P("row", "col"), P("row", "col"), P("row"), P("col"), P()),
        check_vma=False,
    )
```

time: 56.4 us -> 51.1 us (0.906)
  Pallas kernels: 55.7 us -> 50.3 us
    pallas_call x1, Pallas kernels: 52.7 us -> 47.4 us  [body(): pl.pallas_call(functools.partial(exchange_kernel, (rows * 4, cols * 16)),...]
where the time goes in v4:
time: 51.1 us; the launch traced here: 51 us
  Pallas kernels  50.3 us (98%)
  between operations  0.64 us (1%)
    pallas_call x1, Pallas kernels, body(): pl.pallas_call(functools.partial(exchange_kernel, (rows * 4, cols * 16)),...  47.4 us
    pallas_call x1, Pallas kernels, body(): pl.pallas_call(update_kernel, out_shape=(jax.ShapeDtypeStruct((rows, cols...  2.95 us

profile of v4, /device:TPU:1, one launch (start us, length us, event | category | flops | bytes accessed | tf_op | source)
XLA Modules:
  0.0 51.0 jit_solution(17189087327300259102)
XLA Ops:
  0.6 47.4 %exchange.1 = (f32[4,128,1152]{2,1,0:T(8,128)S(1)}, f32[4,128,1152]{2,1,0:T(8,128)S(1)}, f32[1,4608]{1,0:T(1,128)S(1)}, f32[1,128]{1,0:T(1,128)S(1)}, f32[128,12...) custom-call(bf16[1,128,4608]{2,1,0:T(8,128)(2,1)} %grad_hbm.1, f32[128,4608]{1,0:T(8,128)} %weight_hbm.1, ...), custom_call_target="tpu_custom_call" | custom-call | tf_op jit(solution)/shard_map/exchange/pallas_call | solution.py:302
  48.0 3.0 %apply.1 = (f32[128,4608]{1,0:T(8,128)}, f32[128,4608]{1,0:T(8,128)}, f32[128]{0:T(128)}, f32[4608]{0:T(1024)}, f32[1,1]{1,0:T(1,128)}) custom-call(f32[4,128,1152]{2,1,0:T(8,128)S(1)} %get-tuple-element.17.full, f32[4,128,1152]{2,1,0:T(8,128)S(1)} %get-tuple-element.18.held, f32[1,4608]{1,0:T(1,128)S(1)} %get-tuple-element.19.col_all, ...), custom_call_target="tpu_custom_call" | custom-call | tf_op jit(solution)/shard_map/apply/pallas_call | solution.py:328

commit v5 on v4

--- a/solution.py
+++ b/solution.py
@@ -16,7 +16,7 @@
 MESH = pl.DeviceIdType.MESH
 f32 = jnp.float32
 PA, PB, PC, PD, PX, PE = range(6)
-PIECES = (4, 1, 4, 4, 1, 4)
+PIECES = (4, 1, 4, 4, 4, 4)
 
 
 def exchange_kernel(sizes, grad_hbm, weight_hbm, rowm_hbm, colm_hbm,
@@ -63,9 +63,9 @@
                         if which != "r" or i == 0:
                             pl.semaphore_signal(sem, inc=1, device_id=dev, device_id_type=MESH)
 
+    loads[2].start()
     for q in (right, left, opp):
         pl.semaphore_signal(barrier, inc=1, device_id={"dp": q}, device_id_type=MESH)
-    loads[2].start()
     greet(barrier, True)
 
     def at(phase, h, k):
@@ -104,9 +104,12 @@
                 bulk(phase, d, k).wait_send()
 
     loads[2].wait()
-    s_opp[...] = own[2].astype(f32)
-    pl.semaphore_wait(barrier, 3 + 4 * x + place)
     for k in range(PIECES[PA]):
+        for d in range(2):
+            span = at(PA, d, k)
+            s_opp[span] = own[2, span].astype(f32)
+        if k == 0:
+            pl.semaphore_wait(barrier, 3 + 4 * x + place)
         for d in range(2):
             bulk(PA, d, k).start()
     for i in (1, 3, 0, 4, 5, 6, 7, 8, 9):
@@ -186,8 +189,14 @@
     def _():
         pl.semaphore_wait(ready, later)
 
+    def others(first, last):
+        for k in range(first, last):
+            for d in range(2):
+                bulk(PX, d, k).start()
+
     col_parts[r] = jnp.sum(col_acc, axis=0, keepdims=True)
     send_small(0, col_parts, r, [(i, {"row": i}) for i in range(4)])
+    others(0, 1)
     row_sums = jnp.sum(lanes[...].T, axis=0, keepdims=True)
     old = decay_rate * col_old[:, mine]
     whole(0, col_parts, near).wait_recv()
@@ -208,8 +217,7 @@
     raw_sums = jnp.sum(lanes[...].T, axis=0, keepdims=True)
     sums_yx[y * 4 + x] = jnp.concatenate([row_sums, raw_sums, weight_sums, jnp.zeros((5, 128), f32)], axis=0)
     send_small(1, sums_yx, y * 4 + x, [(i * 4 + j, {"dp": i, "col": j * 4 + z}) for i in range(4) for j in range(4)])
-    for d in range(2):
-        bulk(PX, d).start()
+    others(1, PIECES[PX])
     col_all[:, mine] = col_mine
     for q in (right, left, opp):
         pltpu.make_async_remote_copy(
@@ -230,11 +238,15 @@
     col_scale[...] = lax.rsqrt(col_all[...])
     whole(0, col_parts, near).wait_send()
     whole(1, sums_yx, {"dp": right}).wait_send()
-    for phase in (PB, PC, PD, PX, PE):
+    for phase in (PB, PC, PD, PX):
         sent(phase)
-    for d in range(2):
-        arrive(PX, d)
-        for k in range(PIECES[PE]):
+    for k in range(PIECES[PX]):
+        for d in range(2):
+            arrive(PX, d, k)
+    last = PIECES[PE] - 1
+    for k in range(last):
+        for d in range(2):
+            bulk(PE, d, k).wait_send()
             arrive(PE, d, k)
     whole(2, sums_zr, near).wait_recv()
 
@@ -258,6 +270,9 @@
     size = learn_rate * jnp.maximum(eps_two, jnp.sqrt(sums[2:3] / entries))
     scal[...] = jnp.concatenate(
         [jnp.broadcast_to(v, (1, 128)) for v in (clip, size, jnp.sqrt(row_mean) / clip, clip)], axis=0)
+    for d in range(2):
+        bulk(PE, d, last).wait_send()
+        arrive(PE, d, last)
     whole(2, sums_zr, near).wait_send()
 
 

time: 51.1 us -> 49.7 us (0.973)
  Pallas kernels: 50.3 us -> 48.8 us
    pallas_call x1, Pallas kernels: 47.4 us -> 45.8 us  [body(): pl.pallas_call(functools.partial(exchange_kernel, (rows * 4, cols * 16)),...]
where the time goes in v5:
time: 49.7 us; the launch traced here: 49.4 us
  Pallas kernels  48.8 us (98%)
  between operations  0.64 us (1%)
    pallas_call x1, Pallas kernels, body(): pl.pallas_call(functools.partial(exchange_kernel, (rows * 4, cols * 16)),...  45.8 us
    pallas_call x1, Pallas kernels, body(): pl.pallas_call(update_kernel, out_shape=(jax.ShapeDtypeStruct((rows, cols...  2.95 us

profile of v5, /device:TPU:1, one launch (start us, length us, event | category | flops | bytes accessed | tf_op | source)
XLA Modules:
  0.0 49.4 jit_solution(10903307751670067616)
XLA Ops:
  0.6 45.8 %exchange.1 = (f32[4,128,1152]{2,1,0:T(8,128)S(1)}, f32[4,128,1152]{2,1,0:T(8,128)S(1)}, f32[1,4608]{1,0:T(1,128)S(1)}, f32[1,128]{1,0:T(1,128)S(1)}, f32[128,12...) custom-call(bf16[1,128,4608]{2,1,0:T(8,128)(2,1)} %grad_hbm.1, f32[128,4608]{1,0:T(8,128)} %weight_hbm.1, ...), custom_call_target="tpu_custom_call" | custom-call | tf_op jit(solution)/shard_map/exchange/pallas_call | solution.py:317
  46.5 3.0 %apply.1 = (f32[128,4608]{1,0:T(8,128)}, f32[128,4608]{1,0:T(8,128)}, f32[128]{0:T(128)}, f32[4608]{0:T(1024)}, f32[1,1]{1,0:T(1,128)}) custom-call(f32[4,128,1152]{2,1,0:T(8,128)S(1)} %get-tuple-element.17.full, f32[4,128,1152]{2,1,0:T(8,128)S(1)} %get-tuple-element.18.held, f32[1,4608]{1,0:T(1,128)S(1)} %get-tuple-element.19.col_all, ...), custom_call_target="tpu_custom_call" | custom-call | tf_op jit(solution)/shard_map/apply/pallas_call | solution.py:343

commit v6 on v5

--- a/solution.py
+++ b/solution.py
@@ -16,7 +16,7 @@
 MESH = pl.DeviceIdType.MESH
 f32 = jnp.float32
 PA, PB, PC, PD, PX, PE = range(6)
-PIECES = (4, 1, 4, 4, 4, 4)
+PIECES = (2, 1, 2, 2, 4, 2)
 
 
 def exchange_kernel(sizes, grad_hbm, weight_hbm, rowm_hbm, colm_hbm,
@@ -33,7 +33,14 @@
     right, opp, left = lax.rem(y + 1, 4), lax.rem(y + 2, 4), lax.rem(y + 3, 4)
 
     loads = {}
-    for slot, q in ((2, opp), (1, right), (3, left), (0, y)):
+    def first_rows(i):
+        step = half // PIECES[PA]
+        return pl.ds((i % 2) * half + (0 if i < 2 else step), step if i < 2 else half - step)
+
+    cols = pl.ds(pl.multiple_of(opp * width, 128), width)
+    firsts = [pltpu.make_async_copy(
+        grad_hbm.at[0, first_rows(i), cols], own.at[2, first_rows(i)], load_sem.at[(2, 10, 11, 12)[i]]) for i in range(4)]
+    for slot, q in ((1, right), (3, left), (0, y)):
         loads[slot] = pltpu.make_async_copy(
             grad_hbm.at[0, :, pl.ds(pl.multiple_of(q * width, 128), width)], own.at[slot], load_sem.at[slot])
     for q in range(4):
@@ -53,17 +60,17 @@
 
                 @pl.when((to < 4) if later else (to >= 0))
                 def _():
-                    for i in range(4):
+                    for i in range(4 if which == "z" else 1):
                         if which == "x":
-                            dev = {"dp": i, "col": to * 4 + z}
+                            dev = {"col": to * 4 + z}
                         elif which == "z":
                             dev = {"col": x * 4 + to, "row": i}
                         else:
                             dev = {"row": to}
-                        if which != "r" or i == 0:
-                            pl.semaphore_signal(sem, inc=1, device_id=dev, device_id_type=MESH)
-
-    loads[2].start()
+                        pl.semaphore_signal(sem, inc=1, device_id=dev, device_id_type=MESH)
+
+    for copy in firsts:
+        copy.start()
     for q in (right, left, opp):
         pl.semaphore_signal(barrier, inc=1, device_id={"dp": q}, device_id_type=MESH)
     greet(barrier, True)
@@ -103,13 +110,14 @@
             for d in range(2):
                 bulk(phase, d, k).wait_send()
 
-    loads[2].wait()
     for k in range(PIECES[PA]):
+        for copy in (firsts[:2], firsts[2:], (), ())[k]:
+            copy.wait()
         for d in range(2):
             span = at(PA, d, k)
             s_opp[span] = own[2, span].astype(f32)
         if k == 0:
-            pl.semaphore_wait(barrier, 3 + 4 * x + place)
+            pl.semaphore_wait(barrier, 3 + x + place)
         for d in range(2):
             bulk(PA, d, k).start()
     for i in (1, 3, 0, 4, 5, 6, 7, 8, 9):
@@ -183,7 +191,7 @@
         return out
 
     near = {"row": lax.rem(r + 1, 4)}
-    later = 12 - 4 * x + 15 - place
+    later = 3 - x + 15 - place
 
     @pl.when(later > 0)
     def _():
@@ -278,11 +286,17 @@
 
 def update_kernel(full, held, col_all, row_new, row_scale, col_scale, scal,
                   weight_out, update_out, row_out, col_out, clip_out,
-                  new_weight, update, sem):
+                  new_weight, update, row_flat, col_flat, clip_flat, sem, small_sem):
     rows, width = full.shape[1], full.shape[2]
+    row_flat[...] = row_new[...].reshape(row_flat.shape)
+    col_flat[...] = col_all[...].reshape(col_flat.shape)
+    clip_flat[...] = scal[0:1, 0:1]
     size, factor = scal[1:2, :], scal[2:3, :]
     step = 16
-    copies = []
+    copies = [pltpu.make_async_copy(src, dst, small_sem.at[i]) for i, (src, dst) in enumerate(
+        ((row_flat, row_out), (col_flat, col_out), (clip_flat, clip_out)))]
+    for copy in copies:
+        copy.start()
     for k in range(rows // step):
         for i in range(step // 8):
             at = pl.ds(k * step + i * 8, 8)
@@ -298,9 +312,6 @@
         for which, (src, dst) in enumerate(((update, update_out), (new_weight, weight_out))):
             copies.append(pltpu.make_async_copy(src.at[at], dst.at[at], sem.at[which, k]))
             copies[-1].start()
-    row_out[...] = row_new[...].reshape(row_out.shape)
-    col_out[...] = col_all[...].reshape(col_out.shape)
-    clip_out[...] = scal[0:1, 0:1]
     for copy in copies:
         copy.wait()
 
@@ -329,7 +340,7 @@
                 pltpu.VMEM((4, 1, width), f32),
                 pltpu.VMEM((16, 8, 128), f32),
                 pltpu.VMEM((16, 8, 128), f32),
-                pltpu.SemaphoreType.DMA((10,)),
+                pltpu.SemaphoreType.DMA((13,)),
                 pltpu.SemaphoreType.DMA((6, 2, max(PIECES))),
                 pltpu.SemaphoreType.DMA((6, 2, max(PIECES))),
                 pltpu.SemaphoreType.DMA((4,)),
@@ -350,11 +361,15 @@
                 jax.ShapeDtypeStruct((1, 1), f32),
             ),
             in_specs=[vmem] * len(shapes),
-            out_specs=(pl.BlockSpec(memory_space=pl.ANY), pl.BlockSpec(memory_space=pl.ANY), vmem, vmem, vmem),
+            out_specs=(pl.BlockSpec(memory_space=pl.ANY),) * 5,
             scratch_shapes=[
                 pltpu.VMEM((rows, cols), f32),
                 pltpu.VMEM((rows, cols), f32),
+                pltpu.VMEM((rows,), f32),
+                pltpu.VMEM((cols,), f32),
+                pltpu.VMEM((1, 1), f32),
                 pltpu.SemaphoreType.DMA((2, rows // 16)),
+                pltpu.SemaphoreType.DMA((3,)),
             ],
             compiler_params=pltpu.CompilerParams(vmem_limit_bytes=24 << 20),
             name="apply",

time: 49.7 us -> 49.2 us (0.990)
  Pallas kernels: 48.8 us -> 48.1 us
    pallas_call x1, Pallas kernels: 2.95 us -> 2.39 us  [body(): pl.pallas_call(update_kernel, out_shape=(jax.ShapeDtypeStruct((rows, cols...]
where the time goes in v6:
time: 49.2 us; the launch traced here: 48.7 us
  Pallas kernels  48.1 us (98%)
  between operations  0.64 us (1%)
    pallas_call x1, Pallas kernels, body(): pl.pallas_call(functools.partial(exchange_kernel, (rows * 4, cols * 16)),...  45.7 us
    pallas_call x1, Pallas kernels, body(): pl.pallas_call(update_kernel, out_shape=(jax.ShapeDtypeStruct((rows, cols...  2.39 us

profile of v6, /device:TPU:1, one launch (start us, length us, event | category | flops | bytes accessed | tf_op | source)
XLA Modules:
  0.0 48.7 jit_solution(3968353677591170167)
XLA Ops:
  0.6 45.7 %exchange.1 = (f32[4,128,1152]{2,1,0:T(8,128)S(1)}, f32[4,128,1152]{2,1,0:T(8,128)S(1)}, f32[1,4608]{1,0:T(1,128)S(1)}, f32[1,128]{1,0:T(1,128)S(1)}, f32[128,12...) custom-call(bf16[1,128,4608]{2,1,0:T(8,128)(2,1)} %grad_hbm.1, f32[128,4608]{1,0:T(8,128)} %weight_hbm.1, ...), custom_call_target="tpu_custom_call" | custom-call | tf_op jit(solution)/shard_map/exchange/pallas_call | solution.py:328
  46.4 2.4 %apply.1 = (f32[128,4608]{1,0:T(8,128)}, f32[128,4608]{1,0:T(8,128)}, f32[128]{0:T(128)}, f32[4608]{0:T(1024)}, f32[1,1]{1,0:T(1,128)}) custom-call(f32[4,128,1152]{2,1,0:T(8,128)S(1)} %get-tuple-element.17.full, f32[4,128,1152]{2,1,0:T(8,128)S(1)} %get-tuple-element.18.held, f32[1,4608]{1,0:T(1,128)S(1)} %get-tuple-element.19.col_all, ...), custom_call_target="tpu_custom_call" | custom-call | tf_op jit(solution)/shard_map/apply/pallas_call | solution.py:354

commit v7 on v6

--- a/solution.py
+++ b/solution.py
@@ -16,7 +16,8 @@
 MESH = pl.DeviceIdType.MESH
 f32 = jnp.float32
 PA, PB, PC, PD, PX, PE = range(6)
-PIECES = (2, 1, 2, 2, 4, 2)
+EARLY = 24
+PIECES = (2, 1, 2, 2, 2, 2)
 
 
 def exchange_kernel(sizes, grad_hbm, weight_hbm, rowm_hbm, colm_hbm,
@@ -51,31 +52,61 @@
 
     barrier = pltpu.get_barrier_semaphore()
     place = z * 4 + r
-
-    def greet(sem, later):
-        sign = 1 if later else -1
-        for d in range(1, 4):
-            for which, at in (("x", x), ("z", z), ("r", r)):
-                to = at + sign * d
-
-                @pl.when((to < 4) if later else (to >= 0))
-                def _():
-                    for i in range(4 if which == "z" else 1):
-                        if which == "x":
-                            dev = {"col": to * 4 + z}
-                        elif which == "z":
-                            dev = {"col": x * 4 + to, "row": i}
-                        else:
-                            dev = {"row": to}
-                        pl.semaphore_signal(sem, inc=1, device_id=dev, device_id_type=MESH)
-
-    for copy in firsts:
+    hub = 1
+    behind = lax.rem(place + 16 - hub, 16)
+
+    def along_x(sem):
+        for i in range(1, 4):
+            pl.semaphore_signal(sem, inc=1, device_id={"col": i * 4 + z}, device_id_type=MESH)
+
+    def along_z(sem):
+        for i in reversed(range(16)):
+            if i != hub:
+                pl.semaphore_signal(sem, inc=1, device_id={"col": x * 4 + i // 4, "row": i % 4}, device_id_type=MESH)
+
+    def answer():
+        @pl.when(x > 0)
+        def _():
+            pl.semaphore_signal(ready.at[0], inc=1, device_id={"col": z}, device_id_type=MESH)
+
+        @pl.when(behind > 0)
+        def _():
+            pl.semaphore_signal(
+                ready.at[1], inc=1, device_id={"col": x * 4 + hub // 4, "row": hub % 4}, device_id_type=MESH)
+
+    def tell():
+        @pl.when(x == 0)
+        def _():
+            pl.semaphore_wait(ready.at[0], 3)
+            along_x(ready.at[0])
+
+        @pl.when(behind == 0)
+        def _():
+            pl.semaphore_wait(ready.at[1], 15)
+            along_z(ready.at[1])
+
+    def told():
+        @pl.when(x > 0)
+        def _():
+            pl.semaphore_wait(ready.at[0], 1)
+
+        @pl.when(behind > 0)
+        def _():
+            pl.semaphore_wait(ready.at[1], 1)
+
+    for q in (right, left):
+        pl.semaphore_signal(barrier, inc=1, device_id={"dp": q}, device_id_type=MESH)
+    for copy in firsts[:2]:
         copy.start()
-    for q in (right, left, opp):
-        pl.semaphore_signal(barrier, inc=1, device_id={"dp": q}, device_id_type=MESH)
-    greet(barrier, True)
+    pl.semaphore_signal(barrier, inc=1, device_id={"dp": opp}, device_id_type=MESH)
+    for copy in firsts[2:]:
+        copy.start()
+    pl.when(x == 0)(lambda: along_x(barrier))
+    pl.when(behind == 0)(lambda: along_z(barrier))
 
     def at(phase, h, k):
+        if phase == PX:
+            return pl.ds(h * half + (0, EARLY)[k], (EARLY, half - EARLY)[k])
         step = half // PIECES[phase]
         return pl.ds(h * half + k * step, step)
 
@@ -117,7 +148,7 @@
             span = at(PA, d, k)
             s_opp[span] = own[2, span].astype(f32)
         if k == 0:
-            pl.semaphore_wait(barrier, 3 + x + place)
+            pl.semaphore_wait(barrier, 3 + (x + 3) // 4 + (behind + 15) // 16)
         for d in range(2):
             bulk(PA, d, k).start()
     for i in (1, 3, 0, 4, 5, 6, 7, 8, 9):
@@ -128,7 +159,7 @@
         span = at(PB, 1 - d, 0)
         dst[span] = own[slot, span].astype(f32)
         bulk(PB, d).start()
-    greet(ready, False)
+    answer()
     for i in (0, 4, 5, 6, 7, 8, 9):
         loads[i].wait()
 
@@ -151,6 +182,7 @@
             dst[span] = r_opp[span] + own[slot, span].astype(f32)
             bulk(PC, d, k).start()
     sent(PA)
+    tell()
     col_acc = jnp.zeros((8, width), f32)
     arrive(PB, 0)
     arrive(PB, 1)
@@ -191,11 +223,7 @@
         return out
 
     near = {"row": lax.rem(r + 1, 4)}
-    later = 3 - x + 15 - place
-
-    @pl.when(later > 0)
-    def _():
-        pl.semaphore_wait(ready, later)
+    told()
 
     def others(first, last):
         for k in range(first, last):
@@ -226,15 +254,15 @@
     sums_yx[y * 4 + x] = jnp.concatenate([row_sums, raw_sums, weight_sums, jnp.zeros((5, 128), f32)], axis=0)
     send_small(1, sums_yx, y * 4 + x, [(i * 4 + j, {"dp": i, "col": j * 4 + z}) for i in range(4) for j in range(4)])
     others(1, PIECES[PX])
+    for k in range(PIECES[PE]):
+        for d in range(2):
+            arrive(PD, d, k)
+            bulk(PE, d, k).start()
     col_all[:, mine] = col_mine
     for q in (right, left, opp):
         pltpu.make_async_remote_copy(
             src_ref=col_all.at[:, mine], dst_ref=col_all.at[:, mine], send_sem=xs_sem.at[3],
             recv_sem=xr_sem.at[3], device_id={"dp": q}, device_id_type=MESH).start()
-    for k in range(PIECES[PE]):
-        for d in range(2):
-            arrive(PD, d, k)
-            bulk(PE, d, k).start()
     whole(1, sums_yx, {"dp": right}).wait_recv()
     sums_zr[place] = jnp.concatenate([total(sums_yx)[0:3], row_old, jnp.zeros((4, 128), f32)], axis=0)
     send_small(2, sums_zr, place, [(i * 4 + j, {"col": x * 4 + i, "row": j}) for i in range(4) for j in range(4)])
@@ -345,7 +373,7 @@
                 pltpu.SemaphoreType.DMA((6, 2, max(PIECES))),
                 pltpu.SemaphoreType.DMA((4,)),
                 pltpu.SemaphoreType.DMA((4,)),
-                pltpu.SemaphoreType.REGULAR,
+                pltpu.SemaphoreType.REGULAR((2,)),
             ],
             compiler_params=pltpu.CompilerParams(
                 collective_id=0, has_side_effects=True, vmem_limit_bytes=24 << 20),

time: 49.2 us -> 48.5 us (0.986)
  no operation moved by 1% of the time
where the time goes in v7:
time: 48.5 us; the launch traced here: 48.3 us
  Pallas kernels  47.7 us (98%)
  between operations  0.64 us (1%)
    pallas_call x1, Pallas kernels, body(): pl.pallas_call(functools.partial(exchange_kernel, (rows * 4, cols * 16)),...  45.3 us
    pallas_call x1, Pallas kernels, body(): pl.pallas_call(update_kernel, out_shape=(jax.ShapeDtypeStruct((rows, cols...  2.39 us

profile of v7, /device:TPU:1, one launch (start us, length us, event | category | flops | bytes accessed | tf_op | source)
XLA Modules:
  0.0 48.3 jit_solution(6624684339981220513)
XLA Ops:
  0.6 45.3 %exchange.1 = (f32[4,128,1152]{2,1,0:T(8,128)S(1)}, f32[4,128,1152]{2,1,0:T(8,128)S(1)}, f32[1,4608]{1,0:T(1,128)S(1)}, f32[1,128]{1,0:T(1,128)S(1)}, f32[128,12...) custom-call(bf16[1,128,4608]{2,1,0:T(8,128)(2,1)} %grad_hbm.1, f32[128,4608]{1,0:T(8,128)} %weight_hbm.1, ...), custom_call_target="tpu_custom_call" | custom-call | tf_op jit(solution)/shard_map/exchange/pallas_call | solution.py:356
  46.0 2.4 %apply.1 = (f32[128,4608]{1,0:T(8,128)}, f32[128,4608]{1,0:T(8,128)}, f32[128]{0:T(128)}, f32[4608]{0:T(1024)}, f32[1,1]{1,0:T(1,128)}) custom-call(f32[4,128,1152]{2,1,0:T(8,128)S(1)} %get-tuple-element.17.full, f32[4,128,1152]{2,1,0:T(8,128)S(1)} %get-tuple-element.18.held, f32[1,4608]{1,0:T(1,128)S(1)} %get-tuple-element.19.col_all, ...), custom_call_target="tpu_custom_call" | custom-call | tf_op jit(solution)/shard_map/apply/pallas_call | solution.py:382

commit v8 on v7

--- a/solution.py
+++ b/solution.py
@@ -251,7 +251,7 @@
 
     lax.fori_loop(0, rows // 8, raw_step, 0, unroll=4)
     raw_sums = jnp.sum(lanes[...].T, axis=0, keepdims=True)
-    sums_yx[y * 4 + x] = jnp.concatenate([row_sums, raw_sums, weight_sums, jnp.zeros((5, 128), f32)], axis=0)
+    sums_yx[y * 4 + x] = jnp.concatenate([row_sums, raw_sums, weight_sums, jnp.zeros((1, 128), f32)], axis=0)
     send_small(1, sums_yx, y * 4 + x, [(i * 4 + j, {"dp": i, "col": j * 4 + z}) for i in range(4) for j in range(4)])
     others(1, PIECES[PX])
     for k in range(PIECES[PE]):
@@ -264,7 +264,7 @@
             src_ref=col_all.at[:, mine], dst_ref=col_all.at[:, mine], send_sem=xs_sem.at[3],
             recv_sem=xr_sem.at[3], device_id={"dp": q}, device_id_type=MESH).start()
     whole(1, sums_yx, {"dp": right}).wait_recv()
-    sums_zr[place] = jnp.concatenate([total(sums_yx)[0:3], row_old, jnp.zeros((4, 128), f32)], axis=0)
+    sums_zr[place] = jnp.concatenate([total(sums_yx)[0:3], row_old], axis=0)
     send_small(2, sums_zr, place, [(i * 4 + j, {"col": x * 4 + i, "row": j}) for i in range(4) for j in range(4)])
     cols_rest = col_all.at[:, pl.ds(0, 3 * width)]
     cols = pltpu.make_async_remote_copy(
@@ -366,8 +366,8 @@
                 pltpu.VMEM((cols,), f32),
                 pltpu.VMEM((1, cols), f32),
                 pltpu.VMEM((4, 1, width), f32),
-                pltpu.VMEM((16, 8, 128), f32),
-                pltpu.VMEM((16, 8, 128), f32),
+                pltpu.VMEM((16, 4, 128), f32),
+                pltpu.VMEM((16, 4, 128), f32),
                 pltpu.SemaphoreType.DMA((13,)),
                 pltpu.SemaphoreType.DMA((6, 2, max(PIECES))),
                 pltpu.SemaphoreType.DMA((6, 2, max(PIECES))),

time: 48.5 us -> 48.1 us (level)
  no operation moved by 1% of the time
where the time goes in v8:
time: 48.1 us; the launch traced here: 48 us
  Pallas kernels  47.3 us (98%)
  between operations  0.64 us (1%)
    pallas_call x1, Pallas kernels, body(): pl.pallas_call(functools.partial(exchange_kernel, (rows * 4, cols * 16)),...  44.9 us
    pallas_call x1, Pallas kernels, body(): pl.pallas_call(update_kernel, out_shape=(jax.ShapeDtypeStruct((rows, cols...  2.39 us

profile of v8, /device:TPU:1, one launch (start us, length us, event | category | flops | bytes accessed | tf_op | source)
XLA Modules:
  0.0 48.0 jit_solution(10149212100812464192)
XLA Ops:
  0.6 44.9 %exchange.1 = (f32[4,128,1152]{2,1,0:T(8,128)S(1)}, f32[4,128,1152]{2,1,0:T(8,128)S(1)}, f32[1,4608]{1,0:T(1,128)S(1)}, f32[1,128]{1,0:T(1,128)S(1)}, f32[128,12...) custom-call(bf16[1,128,4608]{2,1,0:T(8,128)(2,1)} %grad_hbm.1, f32[128,4608]{1,0:T(8,128)} %weight_hbm.1, ...), custom_call_target="tpu_custom_call" | custom-call | tf_op jit(solution)/shard_map/exchange/pallas_call | solution.py:356
  45.6 2.4 %apply.1 = (f32[128,4608]{1,0:T(8,128)}, f32[128,4608]{1,0:T(8,128)}, f32[128]{0:T(128)}, f32[4608]{0:T(1024)}, f32[1,1]{1,0:T(1,128)}) custom-call(f32[4,128,1152]{2,1,0:T(8,128)S(1)} %get-tuple-element.17.full, f32[4,128,1152]{2,1,0:T(8,128)S(1)} %get-tuple-element.18.held, f32[1,4608]{1,0:T(1,128)S(1)} %get-tuple-element.19.col_all, ...), custom_call_target="tpu_custom_call" | custom-call | tf_op jit(solution)/shard_map/apply/pallas_call | solution.py:382

commit v9 on v8

--- a/solution.py
+++ b/solution.py
@@ -98,7 +98,6 @@
         pl.semaphore_signal(barrier, inc=1, device_id={"dp": q}, device_id_type=MESH)
     for copy in firsts[:2]:
         copy.start()
-    pl.semaphore_signal(barrier, inc=1, device_id={"dp": opp}, device_id_type=MESH)
     for copy in firsts[2:]:
         copy.start()
     pl.when(x == 0)(lambda: along_x(barrier))
@@ -148,7 +147,7 @@
             span = at(PA, d, k)
             s_opp[span] = own[2, span].astype(f32)
         if k == 0:
-            pl.semaphore_wait(barrier, 3 + (x + 3) // 4 + (behind + 15) // 16)
+            pl.semaphore_wait(barrier, 2 + (x + 3) // 4 + (behind + 15) // 16)
         for d in range(2):
             bulk(PA, d, k).start()
     for i in (1, 3, 0, 4, 5, 6, 7, 8, 9):
@@ -159,7 +158,6 @@
         span = at(PB, 1 - d, 0)
         dst[span] = own[slot, span].astype(f32)
         bulk(PB, d).start()
-    answer()
     for i in (0, 4, 5, 6, 7, 8, 9):
         loads[i].wait()
 
@@ -181,6 +179,7 @@
             arrive(PA, d, k)
             dst[span] = r_opp[span] + own[slot, span].astype(f32)
             bulk(PC, d, k).start()
+    answer()
     sent(PA)
     tell()
     col_acc = jnp.zeros((8, width), f32)

time: 48.1 us -> 48 us (level)
  no operation moved by 1% of the time
where the time goes in v9:
time: 48 us; the launch traced here: 47.9 us
  Pallas kernels  47.3 us (99%)
  between operations  0.64 us (1%)
    pallas_call x1, Pallas kernels, body(): pl.pallas_call(functools.partial(exchange_kernel, (rows * 4, cols * 16)),...  44.9 us
    pallas_call x1, Pallas kernels, body(): pl.pallas_call(update_kernel, out_shape=(jax.ShapeDtypeStruct((rows, cols...  2.39 us

profile of v9, /device:TPU:1, one launch (start us, length us, event | category | flops | bytes accessed | tf_op | source)
XLA Modules:
  0.0 47.9 jit_solution(12751017756461248192)
XLA Ops:
  0.6 44.9 %exchange.1 = (f32[4,128,1152]{2,1,0:T(8,128)S(1)}, f32[4,128,1152]{2,1,0:T(8,128)S(1)}, f32[1,4608]{1,0:T(1,128)S(1)}, f32[1,128]{1,0:T(1,128)S(1)}, f32[128,12...) custom-call(bf16[1,128,4608]{2,1,0:T(8,128)(2,1)} %grad_hbm.1, f32[128,4608]{1,0:T(8,128)} %weight_hbm.1, ...), custom_call_target="tpu_custom_call" | custom-call | tf_op jit(solution)/shard_map/exchange/pallas_call | solution.py:355
  45.5 2.4 %apply.1 = (f32[128,4608]{1,0:T(8,128)}, f32[128,4608]{1,0:T(8,128)}, f32[128]{0:T(128)}, f32[4608]{0:T(1024)}, f32[1,1]{1,0:T(1,128)}) custom-call(f32[4,128,1152]{2,1,0:T(8,128)S(1)} %get-tuple-element.17.full, f32[4,128,1152]{2,1,0:T(8,128)S(1)} %get-tuple-element.18.held, f32[1,4608]{1,0:T(1,128)S(1)} %get-tuple-element.19.col_all, ...), custom_call_target="tpu_custom_call" | custom-call | tf_op jit(solution)/shard_map/apply/pallas_call | solution.py:381

commit v10 on v9

--- a/solution.py
+++ b/solution.py
@@ -252,11 +252,12 @@
     raw_sums = jnp.sum(lanes[...].T, axis=0, keepdims=True)
     sums_yx[y * 4 + x] = jnp.concatenate([row_sums, raw_sums, weight_sums, jnp.zeros((1, 128), f32)], axis=0)
     send_small(1, sums_yx, y * 4 + x, [(i * 4 + j, {"dp": i, "col": j * 4 + z}) for i in range(4) for j in range(4)])
-    others(1, PIECES[PX])
     for k in range(PIECES[PE]):
         for d in range(2):
             arrive(PD, d, k)
             bulk(PE, d, k).start()
+        if k == 0:
+            others(1, PIECES[PX])
     col_all[:, mine] = col_mine
     for q in (right, left, opp):
         pltpu.make_async_remote_copy(

time: 48 us -> 48 us (level)
  no operation moved by 1% of the time
where the time goes in v10:
time: 48 us; the launch traced here: 47.9 us
  Pallas kernels  47.3 us (99%)
  between operations  0.64 us (1%)
    pallas_call x1, Pallas kernels, body(): pl.pallas_call(functools.partial(exchange_kernel, (rows * 4, cols * 16)),...  44.9 us
    pallas_call x1, Pallas kernels, body(): pl.pallas_call(update_kernel, out_shape=(jax.ShapeDtypeStruct((rows, cols...  2.39 us

profile of v10, /device:TPU:1, one launch (start us, length us, event | category | flops | bytes accessed | tf_op | source)
XLA Modules:
  0.0 47.9 jit_solution(12946785929236536598)
XLA Ops:
  0.6 44.9 %exchange.1 = (f32[4,128,1152]{2,1,0:T(8,128)S(1)}, f32[4,128,1152]{2,1,0:T(8,128)S(1)}, f32[1,4608]{1,0:T(1,128)S(1)}, f32[1,128]{1,0:T(1,128)S(1)}, f32[128,12...) custom-call(bf16[1,128,4608]{2,1,0:T(8,128)(2,1)} %grad_hbm.1, f32[128,4608]{1,0:T(8,128)} %weight_hbm.1, ...), custom_call_target="tpu_custom_call" | custom-call | tf_op jit(solution)/shard_map/exchange/pallas_call | solution.py:356
  45.5 2.4 %apply.1 = (f32[128,4608]{1,0:T(8,128)}, f32[128,4608]{1,0:T(8,128)}, f32[128]{0:T(128)}, f32[4608]{0:T(1024)}, f32[1,1]{1,0:T(1,128)}) custom-call(f32[4,128,1152]{2,1,0:T(8,128)S(1)} %get-tuple-element.17.full, f32[4,128,1152]{2,1,0:T(8,128)S(1)} %get-tuple-element.18.held, f32[1,4608]{1,0:T(1,128)S(1)} %get-tuple-element.19.col_all, ...), custom_call_target="tpu_custom_call" | custom-call | tf_op jit(solution)/shard_map/apply/pallas_call | solution.py:382
